TPU v7x, 128 devices: a whole 4x4x4 slice. The times are simulated.
128 devices in a mesh: cell: 16 (over x, y), cyc: 2 (over core), feat: 4 (over z).
Axes of the slice: x: 4, y: 4, z: 4, core: 2. Of those that a mesh axis runs over, the one named last changes fastest.
Arguments:
- tensor: float32 [2048, 512, 512], P('cell', 'cyc', 'feat'), may hold values from -750 to 750
- present: int32 [128, 32], P('cell', 'cyc'), may hold values from 0 to 1, as said below
- cyc_factor: float32 [512, 32], P('cyc'), may hold values from -6 to 6
- feat_factor: float32 [512, 32], P('feat'), may hold values from -6 to 6
Outputs:
- cell_unit: float32 [2048, 32], P('cell')
- cyc_unit: float32 [512, 32], P('cyc')
- feat_unit: float32 [512, 32], P('feat')
Inputs may be any that keep to these rules, and one draw needn't show every extreme that they name: `present`: in each row the ones form a prefix of 8 or more blocks; some row is all ones, and some row has exactly 8 ones.
All inputs are finite; a program needn't handle non-finite values.
Results may differ from a plain program's by a relative error of at most 0.00017.
Values sent between devices are 32-bit elements; how exact they have to be, the bound alone decides.
No kernel may reach another device: no remote copies, remote signals or barrier semaphores. Data moves between devices by JAX's collectives and lax.ppermute only.
A program may use at most 128 MiB of HBM per device.

v0:
```python
import jax
import jax.numpy as jnp
from jax import lax
from jax.sharding import PartitionSpec as P

BLK_CELL = 16
BLK_CYC = 16


EPS = 1e-06
HIGHEST_MODE = lax.Precision.HIGHEST


def expand_mask(present):
    spread = jnp.repeat(present.astype(jnp.float32), BLK_CELL, axis=0)
    return jnp.repeat(spread, BLK_CYC, axis=1)


def local_gram(rows):
    return lax.dot_general(rows, rows, (((0,), (0,)), ((), ())), precision=HIGHEST_MODE)


def solve_rows(rhs, gram):
    factor = jnp.linalg.cholesky(gram)
    return jax.scipy.linalg.cho_solve((factor, True), rhs.T).T


def unit_columns(raw, gram, count):
    scale = jnp.sqrt(jnp.diagonal(gram) / count + EPS)
    return (raw / scale, gram / (scale[:, None] * scale[None, :]))


def shards(tensor, present, cyc_factor, feat_factor):
    rows_cell, rows_cyc, rows_feat = tensor.shape
    width = cyc_factor.shape[1]
    cells_all = float(rows_cell * lax.axis_size("cell"))
    cycles_all = float(rows_cyc * lax.axis_size("cyc"))
    feats_all = float(rows_feat * lax.axis_size("feat"))
    recorded = expand_mask(present)
    flat = tensor.reshape(rows_cell * rows_cyc, rows_feat)
    gram_cyc = lax.psum(local_gram(cyc_factor), "cyc")
    gram_feat = lax.psum(local_gram(feat_factor), "feat")
    contracted = jnp.dot(flat, feat_factor, precision=HIGHEST_MODE).reshape(
        rows_cell, rows_cyc, width
    )
    contracted = contracted * recorded[:, :, None]
    part_cell = jnp.einsum("ijr,jr->ir", contracted, cyc_factor, precision=HIGHEST_MODE)
    gram_first = gram_cyc * gram_feat
    summed = lax.psum(part_cell, ("cyc", "feat"))
    raw_cell = solve_rows(summed, gram_first)
    gram_cell = lax.psum(local_gram(raw_cell), "cell")
    cell_unit, unit_gram_cell = unit_columns(raw_cell, gram_cell, cells_all)
    part_cyc = jnp.einsum("ijr,ir->jr", contracted, cell_unit, precision=HIGHEST_MODE)
    gram_second = unit_gram_cell * gram_feat
    summed = lax.psum(part_cyc, ("cell", "feat"))
    raw_cyc = solve_rows(summed, gram_second)
    gram_new = lax.psum(local_gram(raw_cyc), "cyc")
    cyc_unit, unit_gram_cyc = unit_columns(raw_cyc, gram_new, cycles_all)
    joint = cell_unit[:, None, :] * cyc_unit[None, :, :] * recorded[:, :, None]
    part_feat = lax.dot_general(
        flat,
        joint.reshape(rows_cell * rows_cyc, width),
        (((0,), (0,)), ((), ())),
        precision=HIGHEST_MODE,
    )
    gram_third = unit_gram_cell * unit_gram_cyc
    summed = lax.psum(part_feat, ("cell", "cyc"))
    raw_feat = solve_rows(summed, gram_third)
    gram_last = lax.psum(local_gram(raw_feat), "feat")
    feat_unit, unused_gram = unit_columns(raw_feat, gram_last, feats_all)
    return (cell_unit, cyc_unit, feat_unit)


def solution(mesh):
    placed = (P("cell", "cyc", "feat"), P("cell", "cyc"), P("cyc", None), P("feat", None))
    return jax.shard_map(
        shards,
        mesh=mesh,
        in_specs=placed,
        out_specs=(P("cell", None), P("cyc", None), P("feat", None)),
        check_vma=False,
    )
```

profile of v0, /device:TPU:0, one launch (start us, length us, event | category | flops | bytes accessed | tf_op | source)
XLA Modules:
  0.0 680.6 jit_solution(3371364250620891169)
XLA Ops:
  0.6 0.0 copy-start
  0.6 0.7 copy-done
  1.4 0.7 convert_element_type.3
  2.1 0.1 copy.18
  2.2 0.2 fusion.34
  2.3 3.4 psum.56
  5.7 0.9 fusion.35
  6.6 18.3 %psum.57 = f32[32,32]{0,1:T(8,128)S(1)} all-reduce(f32[32,32]{0,1:T(8,128)S(1)} %fusion.35), channel_id=1, replica_groups=mesh['cell'=16,'cyc'=2,'feat'=4] {'feat'}, use_global_device_ids=true, to_apply=%region_1.0 | all-reduce | flops 1024 | bytes 8192 | tf_op jit(solution)/shard_map/psum | solution.py:42
  24.9 0.1 copy.17
  25.0 2.9 cholesky.59
  27.9 0.6 compare_reduce_fusion.2
  28.6 0.7 fusion.14
  29.2 2.4 custom-call.22
  31.7 0.1 broadcast_in_dim.13
  31.8 0.1 reshape.59
  31.9 0.1 copy.19
  32.0 19.9 %convolution_multiply_fusion = f32[128,256,32]{1,2,0:T(8,128)S(1)} fusion(f32[128,256,128]{2,1,0:T(8,128)} %param.7, f32[128,256]{1,0:T(8,128)S(1)} %copy.19, f32[128,32]{0,1:T(8,128)} %param.10), kind=kOutput, calls=%fused_computation.10 | convolution fusion | flops 1611661312 | bytes 21118976 | tf_op jit(solution)/shard_map/dot_general | solution.py:43
  51.9 0.0 copy-start.1
  51.9 1.9 copy-done.1
  53.8 6.0 fusion.5
  59.8 23.6 %psum.58 = f32[32,128]{1,0:T(8,128)S(1)} all-reduce(f32[32,128]{1,0:T(8,128)S(1)} %bitcast.84), channel_id=1, replica_groups=mesh['cell'=16,'cyc'=2,'feat'=4] {'cyc','feat'}, use_global_device_ids=true, to_apply=%region_4.6 | all-reduce | flops 4096 | bytes 32768 | tf_op jit(solution)/shard_map/psum | solution.py:49
  83.4 0.2 fusion.30
  83.6 0.1 fusion.28
  83.7 0.2 fusion.36
  83.9 74.6 %psum.59 = f32[32,32]{0,1:T(8,128)S(1)} all-reduce(f32[32,32]{0,1:T(8,128)S(1)} %fusion.36), channel_id=1, replica_groups=mesh['cell'=16,'cyc'=2,'feat'=4] {'cell'}, use_global_device_ids=true, to_apply=%region_5.8 | all-reduce | flops 1024 | bytes 8192 | tf_op jit(solution)/shard_map/psum | solution.py:51
  158.5 0.7 gather_fusion
  159.2 0.1 fusion.33
  159.3 0.1 fusion.58
  159.4 0.0 copy-start.3
  159.4 0.1 broadcast_divide_fusion
  159.5 6.4 fusion.3
  165.9 343.3 %psum.60 = f32[256,32]{0,1:T(8,128)S(1)} all-reduce(f32[256,32]{0,1:T(8,128)S(1)} %bitcast.82), channel_id=1, replica_groups=mesh['cell'=16,'cyc'=2,'feat'=4] {'cell','feat'}, use_global_device_ids=true, to_apply=%region_6.9 | all-reduce | flops 8192 | bytes 65536 | tf_op jit(solution)/shard_map/psum | solution.py:55
  509.2 0.1 copy.21
  509.3 2.9 cholesky.70
  512.3 0.6 compare_reduce_fusion.1
  512.9 0.7 fusion.15
  513.6 2.4 custom-call.14
  516.0 0.2 fusion.24
  516.2 0.2 fusion.22
  516.4 0.2 fusion.37
  516.6 3.4 psum.61
  519.9 0.7 gather_fusion.1
  520.7 0.1 divide_multiply_fusion
  520.8 0.1 divide_bitcast_fusion
  520.8 0.0 copy-start.2
  520.8 0.1 copy.23
  520.9 2.9 cholesky.81
  523.9 0.6 compare_reduce_fusion
  524.5 0.7 fusion.16
  525.2 2.4 custom-call.23
  527.6 0.1 copy.24
  527.7 12.5 %fusion.10 = f32[32,128]{1,0:T(8,128)S(1)} fusion(f32[128,256,128]{2,1,0:T(8,128)} %param.7, f32[256,32]{0,1:T(8,128)S(1)} %divide_bitcast_fusion, f32[128,32]{1,0:T(8,128)S(1)} %copy.24, f32[128,256]{1,0:T(8,128)S(1)} %copy.19), kind=kOutput, calls=%fused_computation.14 | convolution fusion | flops 1612709888 | bytes 16973824 | tf_op jit(solution)/shard_map/dot_general | solution.py:60
  540.3 0.0 copy-done.3
  540.3 0.0 copy-done.2
  540.3 124.1 %psum.62 = f32[32,128]{1,0:T(8,128)S(1)} all-reduce(f32[32,128]{1,0:T(8,128)S(1)} %fusion.10), channel_id=1, replica_groups=mesh['cell'=16,'cyc'=2,'feat'=4] {'cell','cyc'}, use_global_device_ids=true, to_apply=%region_8.11 | all-reduce | flops 4096 | bytes 32768 | tf_op jit(solution)/shard_map/psum | solution.py:67
  664.4 0.2 fusion.19
  664.6 0.1 fusion.17
  664.7 0.2 fusion.38
  664.9 14.3 %psum.63 = f32[32,32]{1,0:T(8,128)S(1)} all-reduce(f32[32,32]{1,0:T(8,128)S(1)} %fusion.38), channel_id=1, replica_groups=mesh['cell'=16,'cyc'=2,'feat'=4] {'feat'}, use_global_device_ids=true, to_apply=%region_9.12 | all-reduce | flops 1024 | bytes 8192 | tf_op jit(solution)/shard_map/psum | solution.py:69
  679.2 0.7 gather_fusion.2
  679.9 0.7 divide_bitcast_fusion.1
  (13 shorter events, 0.2 us)
Async XLA Ops:
  0.6 0.8 copy-start
  51.9 1.9 copy-start.1
  159.4 380.9 %copy-start.3 = (f32[128,32]{0,1:T(8,128)}, f32[128,32]{0,1:T(8,128)S(1)}, u32[]{:S(2)}) copy-start(f32[128,32]{0,1:T(8,128)S(1)} %fusion.58) | copy-start | bytes 49156
  520.8 19.4 %copy-start.2 = (f32[256,32]{0,1:T(8,128)}, f32[256,32]{0,1:T(8,128)S(1)}, u32[]{:S(2)}) copy-start(f32[256,32]{0,1:T(8,128)S(1)} %divide_bitcast_fusion) | copy-start | bytes 98308
where the time goes:
time: 681 us
  blocking collectives  605 us (89%)
  matrix products  47.5 us (7%)
  other arithmetic  21.9 us (3%)
    psum x1, blocking collectives, shards(): summed = lax.psum(part_cyc, ('cell', 'feat'))  343 us
    psum x1, blocking collectives, shards(): summed = lax.psum(part_feat, ('cell', 'cyc'))  124 us
    psum x1, blocking collectives, shards(): gram_cell = lax.psum(local_gram(raw_cell), 'cell')  74.6 us
    psum x1, blocking collectives, shards(): summed = lax.psum(part_cell, ('cyc', 'feat'))  23.6 us
    dot_general x1, matrix products, shards(): jnp.dot(flat, feat_factor, precision=HIGHEST_MODE)  19.9 us
    psum x1, blocking collectives, shards(): gram_feat = lax.psum(local_gram(feat_factor), 'feat')  18.3 us
    psum x1, blocking collectives, shards(): gram_last = lax.psum(local_gram(raw_feat), 'feat')  14.3 us

commit v1 on v0

v1 whole, which is shorter than its diff:
```python
import functools

import jax
import jax.numpy as jnp
from jax import lax
from jax.experimental import pallas as pl
from jax.experimental.pallas import tpu as pltpu
from jax.sharding import PartitionSpec as P

BLK = 16
EPS = 1e-06
HIGHEST = lax.Precision.HIGHEST
F32 = jnp.float32
BF16 = jnp.bfloat16
VMEM_LIMIT = 48 * 1024 * 1024
LANES = 128


def dot(a, b, dims, precision=None):
    return lax.dot_general(a, b, (dims, ((), ())), precision=precision, preferred_element_type=F32)


def split(x):
    hi = x.astype(BF16)
    return hi, (x - hi.astype(F32)).astype(BF16)


def lane_iota(rows, cols=LANES):
    return lax.broadcasted_iota(jnp.int32, (rows, cols), 1)


def wide_gram(rows_t):
    r, n = rows_t.shape
    padded = jnp.concatenate([rows_t, jnp.zeros((LANES - r, n), F32)], axis=0)
    return dot(rows_t, padded, ((1,), (1,)), HIGHEST)


def pack(wide):
    out = wide[0:8]
    for q in range(1, 4):
        out = out + pltpu.roll(wide[8 * q : 8 * q + 8], 32 * q, 1)
    return out


def unpack(packed):
    used = lane_iota(8) < 32
    parts = [packed if q == 0 else pltpu.roll(packed, LANES - 32 * q, 1) for q in range(4)]
    return jnp.concatenate([jnp.where(used, x, 0.0) for x in parts], axis=0)


def inverse(m):
    r = m.shape[0]
    row_id = lax.broadcasted_iota(jnp.int32, m.shape, 0)
    col_id = lax.broadcasted_iota(jnp.int32, m.shape, 1)
    for p in range(r):
        row = m[p : p + 1, :]
        col = m[:, p : p + 1]
        d = 1.0 / m[p : p + 1, p : p + 1]
        on_col = col_id == p
        row = jnp.where(on_col[0:1], d, row * d)
        m = jnp.where(row_id == p, row, jnp.where(on_col, 0.0, m) - col * row)
    return m


def scales(wide, count):
    r = wide.shape[0]
    row_id = lax.broadcasted_iota(jnp.int32, wide.shape, 0)
    col_id = lax.broadcasted_iota(jnp.int32, wide.shape, 1)
    diag = jnp.where(row_id == col_id, wide, 0.0)
    col = jnp.sqrt(jnp.sum(diag, axis=1, keepdims=True) / count + EPS)
    row = jnp.sqrt(jnp.sum(diag, axis=0, keepdims=True) / count + EPS)
    return col, row


def expand_rows(present):
    nb, mb = present.shape
    first = lax.broadcasted_iota(jnp.int32, (mb, mb * BLK), 0) * BLK
    cyc = lax.broadcasted_iota(jnp.int32, (mb, mb * BLK), 1)
    spread = jnp.where((cyc >= first) & (cyc < first + BLK), 1.0, 0.0)
    return dot(present.astype(F32), spread, ((1,), (0,)), HIGHEST)


def contract_kernel(present, cyc_t, feat_t, tensor, c_out, pay, t_buf, c_buf, mask, lhs, t_sem, c_sem):
    cells = tensor.shape[0]
    chunks = cells // BLK
    rank = cyc_t.shape[0]

    def fetch(n):
        rows = pl.ds(n * BLK, BLK)
        return pltpu.make_async_copy(tensor.at[rows], t_buf.at[rows], t_sem.at[n])

    def flush(n):
        rows = pl.ds(n * BLK, BLK)
        return pltpu.make_async_copy(c_buf.at[rows], c_out.at[rows], c_sem.at[n])

    for n in range(chunks):
        fetch(n).start()
    mask[...] = expand_rows(present[...])
    hi, lo = split(feat_t[...])
    lhs[0:rank, :] = jnp.concatenate([hi, hi], axis=1)
    lhs[rank:, :] = jnp.concatenate([lo, jnp.zeros_like(lo)], axis=1)
    gram_cyc = pack(wide_gram(cyc_t[...]))
    gram_feat = pack(wide_gram(feat_t[...]))
    lane = lane_iota(rank)

    def step(n, part):
        fetch(n).wait()
        row = mask[pl.ds(n, 1), :]
        left = lhs[...]
        for q in range(BLK):
            i = n * BLK + q
            hi, lo = split(t_buf[i])
            out = dot(left, jnp.concatenate([hi, lo], axis=1), ((1,), (1,)))
            c = out[:rank] * row + out[rank:] * row
            c_buf[i] = c
            total = jnp.sum(c * cyc_t[...], axis=1, keepdims=True)
            part = jnp.where(lane == i, total, part)
        flush(n).start()
        return part

    part = lax.fori_loop(0, chunks, step, jnp.zeros((rank, cells), F32))
    for d in range(pay.shape[0]):
        pay[d, 0:rank, :] = part
        pay[d, rank : rank + 8, :] = gram_cyc
        pay[d, rank + 8 :, :] = gram_feat
    for n in range(chunks):
        flush(n).wait()


def cells_kernel(got, c_in, raw_out, gram_feat_out, pay, c_buf, c_sem):
    cells, rank = c_in.shape[0], c_in.shape[1]
    chunks = cells // BLK

    def fetch(n):
        rows = pl.ds(n * BLK, BLK)
        return pltpu.make_async_copy(c_in.at[rows], c_buf.at[rows], c_sem.at[n])

    for n in range(chunks):
        fetch(n).start()
    part = got[0, 0:rank, :]
    for d in range(1, 8):
        part = part + got[d, 0:rank, :]
    gram_cyc = unpack(got[0, rank : rank + 8, :] + got[4, rank : rank + 8, :])
    gram_feat = got[0, rank + 8 :, :]
    for d in range(1, 4):
        gram_feat = gram_feat + got[d, rank + 8 :, :]
    gram_feat = unpack(gram_feat)
    gram_feat_out[...] = gram_feat
    inv = inverse(gram_cyc * gram_feat)
    raw = dot(inv[:, :rank], part, ((1,), (0,)), HIGHEST)
    raw_out[...] = raw
    gram = pack(wide_gram(raw))

    def step(n, carry):
        fetch(n).wait()
        total, rolled = carry
        for q in range(BLK):
            total = total + c_buf[n * BLK + q] * rolled[:, q : q + 1]
        return total, pltpu.roll(rolled, LANES - BLK, 1)

    total, _ = lax.fori_loop(0, chunks, step, (jnp.zeros((rank, c_in.shape[2]), F32), raw))
    for d in range(pay.shape[0]):
        pay[d, 0:rank, :] = total[:, :LANES]
        pay[d, rank : 2 * rank, :] = total[:, LANES:]
        pay[d, 2 * rank :, :] = gram


def spread_kernel(rows, got, pay):
    total = got[0]
    for d in range(1, got.shape[0]):
        total = total + got[d]
    for d in range(pay.shape[0]):
        pay[d, :rows, :] = total[:rows]
        pay[d, rows:, :] = got[0, rows:, :]


def cycles_kernel(
    cells_all, present, got, raw_cell, gram_feat, tensor,
    cell_unit, raw_cyc_out, unit_out, pay, t_buf, mask, raw_cyc, wide, t_sem,
):
    cells = tensor.shape[0]
    chunks = cells // BLK
    rank = raw_cell.shape[0]

    def fetch(n):
        rows = pl.ds(n * BLK, BLK)
        return pltpu.make_async_copy(tensor.at[rows], t_buf.at[rows], t_sem.at[n])

    for n in range(chunks):
        fetch(n).start()
    mask[...] = expand_rows(present[...])
    total = got[0]
    for d in range(1, got.shape[0]):
        total = total + got[d]
    gram = unpack(total[2 * rank :])
    col, row = scales(gram, cells_all)
    unit = gram / (col * row)
    unit_out[...] = unit
    inv = inverse(unit * gram_feat[...])
    for h in range(2):
        half = total[h * rank : (h + 1) * rank] / col
        raw_cyc[:, h * LANES : (h + 1) * LANES] = dot(inv[:, :rank], half, ((1,), (0,)), HIGHEST)
    raw_cyc_out[...] = raw_cyc[...]
    cell_t = raw_cell[...] / col
    cell_unit[...] = cell_t

    def step(n, carry):
        acc, rolled = carry
        fetch(n).wait()
        hi, lo = split(raw_cyc[...] * mask[pl.ds(n, 1), :])
        left = jnp.concatenate([hi, lo], axis=0)
        for q in range(BLK):
            hi, lo = split(t_buf[n * BLK + q])
            wide[q] = dot(left, jnp.concatenate([hi, lo], axis=1), ((1,), (0,)))
        for q in range(BLK):
            w = wide[q, :rank, :LANES] + (wide[q, :rank, LANES:] + wide[q, rank:, :LANES])
            acc = acc + w * rolled[:, q : q + 1]
        return acc, pltpu.roll(rolled, LANES - BLK, 1)

    acc, _ = lax.fori_loop(0, chunks, step, (jnp.zeros((rank, LANES), F32), cell_t))
    pay[0:rank, :] = acc
    pay[rank:, :] = pack(wide_gram(raw_cyc[...]))


def pair_kernel(mine, other, pay):
    total = mine[...] + other[...]
    for d in range(pay.shape[0]):
        pay[d] = total


def feats_kernel(cycles_all, got, raw_cyc, unit_cell, cyc_unit, raw_out, pay):
    rank = raw_cyc.shape[0]
    total = got[0]
    for d in range(1, got.shape[0]):
        total = total + got[d]
    gram = unpack(got[0, rank:, :])
    col, row = scales(gram, cycles_all)
    inv = inverse(unit_cell[...] * (gram / (col * row)))
    raw = dot(inv[:, :rank], total[:rank] / col, ((1,), (0,)), HIGHEST)
    raw_out[...] = raw
    square = jnp.broadcast_to(jnp.sum(raw * raw, axis=1, keepdims=True), (rank, LANES))
    for d in range(pay.shape[0]):
        pay[d] = square
    cyc_unit[...] = raw_cyc[...] / col


def last_kernel(feats_all, got, raw, feat_unit):
    total = got[0]
    for d in range(1, got.shape[0]):
        total = total + got[d]
    feat_unit[...] = raw[...] / jnp.sqrt(total / feats_all + EPS)


def shape(*dims):
    return jax.ShapeDtypeStruct(dims, F32)


PARAMS = pltpu.CompilerParams(vmem_limit_bytes=VMEM_LIMIT)
ANY = pl.BlockSpec(memory_space=pl.ANY)
VMEM = pl.BlockSpec(memory_space=pltpu.VMEM)


def shards(tensor, present, cyc_factor, feat_factor):
    cells, cycles, feats = tensor.shape
    rank = cyc_factor.shape[1]
    chunks = cells // BLK
    n_cell, n_cyc, n_feat = (lax.axis_size(a) for a in ("cell", "cyc", "feat"))
    c, pay = pl.pallas_call(
        contract_kernel,
        out_shape=(shape(cells, rank, cycles), shape(n_cyc * n_feat, rank + 16, LANES)),
        in_specs=[VMEM, VMEM, VMEM, ANY],
        out_specs=(ANY, VMEM),
        scratch_shapes=[
            pltpu.VMEM((cells, cycles, feats), F32),
            pltpu.VMEM((cells, rank, cycles), F32),
            pltpu.VMEM((chunks, cycles), F32),
            pltpu.VMEM((2 * rank, 2 * feats), BF16),
            pltpu.SemaphoreType.DMA((chunks,)),
            pltpu.SemaphoreType.DMA((chunks,)),
        ],
        compiler_params=PARAMS,
        name="contract",
    )(present, cyc_factor.T, feat_factor.T, tensor)
    got = lax.all_to_all(pay, ("cyc", "feat"), 0, 0)
    raw_cell, gram_feat, pay = pl.pallas_call(
        cells_kernel,
        out_shape=(shape(rank, cells), shape(rank, LANES), shape(n_feat, 2 * rank + 8, LANES)),
        in_specs=[VMEM, ANY],
        out_specs=(VMEM, VMEM, VMEM),
        scratch_shapes=[pltpu.VMEM((cells, rank, cycles), F32), pltpu.SemaphoreType.DMA((chunks,))],
        compiler_params=PARAMS,
        name="cells",
    )(got, c)
    got = lax.all_to_all(pay, "feat", 0, 0)
    pay = pl.pallas_call(
        functools.partial(spread_kernel, 2 * rank),
        out_shape=shape(n_cell, 2 * rank + 8, LANES),
        name="spread",
    )(got)
    got = lax.all_to_all(pay, "cell", 0, 0)
    cell_unit, raw_cyc, unit_cell, pay = pl.pallas_call(
        functools.partial(cycles_kernel, float(cells * n_cell)),
        out_shape=(shape(rank, cells), shape(rank, cycles), shape(rank, LANES), shape(rank + 8, LANES)),
        in_specs=[VMEM, VMEM, VMEM, VMEM, ANY],
        out_specs=(VMEM, VMEM, VMEM, VMEM),
        scratch_shapes=[
            pltpu.VMEM((cells, cycles, feats), F32),
            pltpu.VMEM((chunks, cycles), F32),
            pltpu.VMEM((rank, cycles), F32),
            pltpu.VMEM((BLK, 2 * rank, 2 * feats), F32),
            pltpu.SemaphoreType.DMA((chunks,)),
        ],
        compiler_params=PARAMS,
        name="cycles",
    )(present, got, raw_cell, gram_feat, tensor)
    other = lax.ppermute(pay, "cyc", [(i, n_cyc - 1 - i) for i in range(n_cyc)])
    pay = pl.pallas_call(pair_kernel, out_shape=shape(n_cell, rank + 8, LANES), name="pair")(pay, other)
    got = lax.all_to_all(pay, "cell", 0, 0)
    cyc_unit, raw_feat, pay = pl.pallas_call(
        functools.partial(feats_kernel, float(cycles * n_cyc)),
        out_shape=(shape(rank, cycles), shape(rank, feats), shape(n_feat, rank, LANES)),
        name="feats",
    )(got, raw_cyc, unit_cell)
    got = lax.all_to_all(pay, "feat", 0, 0)
    feat_unit = pl.pallas_call(
        functools.partial(last_kernel, float(feats * n_feat)),
        out_shape=shape(rank, feats),
        name="last",
    )(got, raw_feat)
    return cell_unit.T, cyc_unit.T, feat_unit.T


def solution(mesh):
    placed = (P("cell", "cyc", "feat"), P("cell", "cyc"), P("cyc", None), P("feat", None))
    return jax.shard_map(
        shards,
        mesh=mesh,
        in_specs=placed,
        out_specs=(P("cell", None), P("cyc", None), P("feat", None)),
        check_vma=False,
    )
```

time: 681 us -> 99.3 us (0.15)
  blocking collectives: 605 us -> 62.5 us
  matrix products: 47.5 us -> 0 us
  Pallas kernels: 0 us -> 30.2 us
  other arithmetic: 21.9 us -> 0 us
    psum x8 -> x0, blocking collectives: 605 us -> none  [the longest x1 343 us: shards(): summed = lax.psum(part_cyc, ('cell', 'feat'))]
    all_to_all x0 -> x5, blocking collectives: none -> 62.5 us  [the longest x2 32.3 us: shards(): got = lax.all_to_all(pay, 'cell', 0, 0)]
    dot_general x9 -> x0, matrix products: 46.4 us -> none  [the longest x1 19.9 us: shards(): jnp.dot(flat, feat_factor, precision=HIGHEST_MODE)]
    pallas_call x0 -> x7, Pallas kernels: none -> 30.2 us  [the longest x1 8.85 us: shards(): pl.pallas_call(contract_kernel, out_shape=(shape(cells, rank, cycles), sh...]
    another operation x15 -> x0, other arithmetic: 20 us -> none  [the longest x9 10.8 us: solve_rows(): factor = jnp.linalg.cholesky(gram)]
  transfers between devices with their start and end apart: 0 -> 1, of which waited for: 0 -> 1; matrix products, arithmetic and copies ran while one was open for 0% -> 0% of each run, Pallas kernels for 0% -> 0%
where the time goes in v1:
time: 99.3 us; the launch traced here: 98.5 us
  blocking collectives  62.5 us (63%)
  Pallas kernels  30.2 us (30%)
  local copies, waits for them, and re-layouts  3.97 us (4%)
  waiting for transfers between devices  1.19 us (1%)
    all_to_all x2, blocking collectives, shards(): got = lax.all_to_all(pay, 'cell', 0, 0)  32.3 us
    all_to_all x2, blocking collectives, shards(): got = lax.all_to_all(pay, 'feat', 0, 0)  18.7 us
    all_to_all x1, blocking collectives, shards(): got = lax.all_to_all(pay, ('cyc', 'feat'), 0, 0)  11.5 us
    pallas_call x1, Pallas kernels, shards(): pl.pallas_call(contract_kernel, out_shape=(shape(cells, rank, cycles), sh...  8.85 us
    pallas_call x1, Pallas kernels, shards(): pl.pallas_call(functools.partial(cycles_kernel, float(cells * n_cell)), o...  7.23 us
    pallas_call x1, Pallas kernels, shards(): pl.pallas_call(cells_kernel, out_shape=(shape(rank, cells), shape(rank, L...  4.74 us
    pallas_call x1, Pallas kernels, shards(): pl.pallas_call(functools.partial(feats_kernel, float(cycles * n_cyc)), ou...  4.66 us
    unnamed x16, local copies, waits for them, and re-layouts  3.97 us
  transfers between devices with their start and end apart: 1, of which 1 were waited for; matrix products, arithmetic and copies ran while one was open for 0% of the time, Pallas kernels for 0%

profile of v1, /device:TPU:0, one launch (start us, length us, event | category | flops | bytes accessed | tf_op | source)
XLA Modules:
  0.0 98.5 jit_solution(11664542292187064594)
XLA Ops:
  0.6 0.0 copy-start
  0.6 0.7 copy-done
  1.4 0.0 copy-start.4
  1.4 0.7 copy-done.4
  2.1 0.0 copy-start.5
  2.1 0.7 copy-done.5
  2.8 0.0 copy-start.6
  2.8 8.8 %contract.1 = (f32[128,32,256]{2,1,0:T(8,128)S(1)}, f32[8,48,128]{2,1,0:T(8,128)S(1)}) custom-call(s32[8,16]{1,0:T(8,128)S(1)} %copy-done.5, f32[32,256]{1,0:T(8,128)S(1)} %bitcast.5, f32[32,128]{1,0:T(8,128)S(1)} %bitcast.6, f32[128,256,128]{2,1,0:T(8,128)} %tensor.3), custom_call_target="tpu_custom_call" | custom-call | tf_op jit(solution)/shard_map/contract/pallas_call | solution.py:268
  11.7 11.5 %all_to_all.25.got = f32[8,48,128]{2,1,0:T(8,128)S(1)} all-to-all(f32[8,48,128]{2,1,0:T(8,128)S(1)} %get-tuple-element.15), channel_id=1, replica_groups=mesh['cell'=16,'cyc'=2,'feat'=4] {'cyc','feat'}, dimensions={0} | all-to-all | bytes 393216 | tf_op jit(solution)/shard_map/all_to_all | solution.py:284
  23.1 4.7 %cells.1 = (f32[32,128]{1,0:T(8,128)S(1)}, f32[32,128]{1,0:T(8,128)S(1)}, f32[4,72,128]{2,1,0:T(8,128)S(1)}) custom-call(f32[8,48,128]{2,1,0:T(8,128)S(1)} %all_to_all.25.got, f32[128,32,256]{2,1,0:T(8,128)S(1)} %get-tuple-element.16.c_in), custom_call_target="tpu_custom_call" | custom-call | tf_op jit(solution)/shard_map/cells/pallas_call | solution.py:285
  27.9 9.1 %all_to_all.26.got = f32[4,72,128]{2,1,0:T(8,128)} all-to-all(f32[4,72,128]{2,1,0:T(8,128)S(1)} %get-tuple-element.17), channel_id=1, replica_groups=mesh['cell'=16,'cyc'=2,'feat'=4] {'feat'}, dimensions={0} | all-to-all | bytes 294912 | tf_op jit(solution)/shard_map/all_to_all | solution.py:294
  37.0 1.8 %spread.1 = f32[16,72,128]{2,1,0:T(8,128)} custom-call(f32[4,72,128]{2,1,0:T(8,128)} %all_to_all.26.got), custom_call_target="tpu_custom_call" | custom-call | tf_op jit(solution)/shard_map/spread/pallas_call | solution.py:295
  38.8 18.4 %all_to_all.27.got = f32[16,72,128]{2,1,0:T(8,128)S(1)} all-to-all(f32[16,72,128]{2,1,0:T(8,128)} %spread.1), channel_id=1, replica_groups=mesh['cell'=16,'cyc'=2,'feat'=4] {'cell'}, dimensions={0} | all-to-all | bytes 1179648 | tf_op jit(solution)/shard_map/all_to_all | solution.py:300
  57.1 0.0 copy-done.6
  57.1 7.2 %cycles.1 = (f32[32,128]{1,0:T(8,128)}, f32[32,256]{1,0:T(8,128)S(1)}, f32[32,128]{1,0:T(8,128)S(1)}, f32[40,128]{1,0:T(8,128)S(1)}) custom-call(s32[8,16]{1,0:T(8,128)S(1)} %copy-done.6, f32[16,72,128]{2,1,0:T(8,128)S(1)} %all_to_all.27.got, f32[32,128]{1,0:T(8,128)S(1)} %get-tuple-element.18.raw_cell, f32[32,128]{1,0:T(8,128)S(1)} %get-tuple-element.19.gram_feat, ...), custom_call_target="tpu_custom_call" | custom-call | tf_op jit(solution)/shard_map/cycles/pallas_call | solution.py:301
  64.4 0.0 copy-start.1
  64.4 0.6 copy-done.1
  65.0 0.0 copy-start.3
  65.0 0.6 copy-done.3
  65.6 0.0 copy-start.2
  65.6 0.0 collective-permute-start
  65.6 1.2 %collective-permute-done.other = f32[40,128]{1,0:T(8,128)S(1)} collective-permute-done((f32[40,128]{1,0:T(8,128)S(1)}, f32[40,128]{1,0:T(8,128)S(1)}, u32[]{:S(2)}, u32[]{:S(2)}) %collective-permute-start) | collective-permute-done | bytes 20512 | tf_op jit(solution)/shard_map/ppermute | solution.py:316
  66.8 0.0 copy-done.2
  66.8 0.0 copy-start.7
  66.8 0.6 copy-done.7
  67.4 1.5 %pair.1 = f32[16,40,128]{2,1,0:T(8,128)} custom-call(f32[40,128]{1,0:T(8,128)} %copy-done.2, f32[40,128]{1,0:T(8,128)} %copy-done.7), custom_call_target="tpu_custom_call" | custom-call | tf_op jit(solution)/shard_map/pair/pallas_call | solution.py:317
  68.9 13.9 %all_to_all.28.got = f32[16,40,128]{2,1,0:T(8,128)} all-to-all(f32[16,40,128]{2,1,0:T(8,128)} %pair.1), channel_id=1, replica_groups=mesh['cell'=16,'cyc'=2,'feat'=4] {'cell'}, dimensions={0} | all-to-all | bytes 655360 | tf_op jit(solution)/shard_map/all_to_all | solution.py:318
  82.8 4.7 %feats.1 = (f32[32,256]{1,0:T(8,128)}, f32[32,128]{1,0:T(8,128)}, f32[4,32,128]{2,1,0:T(8,128)}) custom-call(f32[16,40,128]{2,1,0:T(8,128)} %all_to_all.28.got, f32[32,256]{1,0:T(8,128)} %copy-done.1, f32[32,128]{1,0:T(8,128)} %copy-done.3), custom_call_target="tpu_custom_call" | custom-call | tf_op jit(solution)/shard_map/feats/pallas_call | solution.py:319
  87.5 9.6 %all_to_all.29.got = f32[4,32,128]{2,1,0:T(8,128)} all-to-all(f32[4,32,128]{2,1,0:T(8,128)} %get-tuple-element.25), channel_id=1, replica_groups=mesh['cell'=16,'cyc'=2,'feat'=4] {'feat'}, dimensions={0} | all-to-all | bytes 131072 | tf_op jit(solution)/shard_map/all_to_all | solution.py:324
  97.1 1.5 %last.1 = f32[32,128]{1,0:T(8,128)} custom-call(f32[4,32,128]{2,1,0:T(8,128)} %all_to_all.29.got, f32[32,128]{1,0:T(8,128)} %get-tuple-element.26.raw), custom_call_target="tpu_custom_call" | custom-call | tf_op jit(solution)/shard_map/last/pallas_call | solution.py:325
Async XLA Ops:
  0.6 0.8 copy-start
  1.4 0.7 copy-start.4
  2.1 0.7 copy-start.5
  2.8 54.4 %copy-start.6 = (s32[8,16]{1,0:T(8,128)S(1)}, s32[8,16]{1,0:T(8,128)}, u32[]{:S(2)}) copy-start(s32[8,16]{1,0:T(8,128)} %present.3) | copy-start | bytes 1540
  64.4 0.6 copy-start.1
  65.0 0.6 copy-start.3
  65.6 1.2 %copy-start.2 = (f32[40,128]{1,0:T(8,128)}, f32[40,128]{1,0:T(8,128)S(1)}, u32[]{:S(2)}) copy-start(f32[40,128]{1,0:T(8,128)S(1)} %get-tuple-element.21.mine) | copy-start | bytes 61444
  65.6 1.2 %collective-permute-start = (f32[40,128]{1,0:T(8,128)S(1)}, f32[40,128]{1,0:T(8,128)S(1)}, u32[]{:S(2)}, u32[]{:S(2)}) collective-permute-start(f32[40,128]{1,0:T(8,128)S(1)} %get-tuple-element.21.mine), channel_id=1, source_target_pairs={{0,4},{4,0},{1,5},{5,1},{2,6},{6,2},{3,7},{7,3},{8,12},{12,8},{9,1... | collective-permute-start | bytes 61448 | tf_op jit(solution)/shard_map/ppermute | solution.py:316
  66.8 0.6 copy-start.7

commit v2 on v1

--- a/solution.py
+++ b/solution.py
@@ -48,17 +48,21 @@
     return jnp.concatenate([jnp.where(used, x, 0.0) for x in parts], axis=0)
 
 
-def inverse(m):
-    r = m.shape[0]
+def inverse(m, width=16):
     row_id = lax.broadcasted_iota(jnp.int32, m.shape, 0)
     col_id = lax.broadcasted_iota(jnp.int32, m.shape, 1)
-    for p in range(r):
-        row = m[p : p + 1, :]
-        col = m[:, p : p + 1]
-        d = 1.0 / m[p : p + 1, p : p + 1]
-        on_col = col_id == p
-        row = jnp.where(on_col[0:1], d, row * d)
-        m = jnp.where(row_id == p, row, jnp.where(on_col, 0.0, m) - col * row)
+    for start in range(0, m.shape[0], width):
+        cols = [jnp.broadcast_to(m[:, start + k : start + k + 1], m.shape) for k in range(width)]
+        for k in range(width):
+            p = start + k
+            col = cols[k]
+            d = 1.0 / col[p : p + 1, :]
+            row = jnp.where(col_id[0:1] == p, d, m[p : p + 1, :] * d)
+            here = row_id == p
+            m = jnp.where(here, row, jnp.where(col_id == p, 0.0, m) - col * row)
+            for q in range(k + 1, width):
+                f = cols[q][p : p + 1, :] * d
+                cols[q] = jnp.where(here, f, cols[q] - col * f)
     return m
 
 
@@ -80,10 +84,16 @@
     return dot(present.astype(F32), spread, ((1,), (0,)), HIGHEST)
 
 
-def contract_kernel(present, cyc_t, feat_t, tensor, c_out, pay, t_buf, c_buf, mask, lhs, t_sem, c_sem):
+def contract_kernel(
+    present_in, cyc_in, feat_in, tensor, c_out, pay, t_buf, c_buf, present, cyc_t, feat_t, mask, lhs, t_sem, c_sem, in_sem
+):
     cells = tensor.shape[0]
     chunks = cells // BLK
     rank = cyc_t.shape[0]
+    small = [
+        pltpu.make_async_copy(src, dst, in_sem.at[n])
+        for n, (src, dst) in enumerate(((present_in, present), (cyc_in, cyc_t), (feat_in, feat_t)))
+    ]
 
     def fetch(n):
         rows = pl.ds(n * BLK, BLK)
@@ -93,8 +103,12 @@
         rows = pl.ds(n * BLK, BLK)
         return pltpu.make_async_copy(c_buf.at[rows], c_out.at[rows], c_sem.at[n])
 
+    for copy in small:
+        copy.start()
     for n in range(chunks):
         fetch(n).start()
+    for copy in small:
+        copy.wait()
     mask[...] = expand_rows(present[...])
     hi, lo = split(feat_t[...])
     lhs[0:rank, :] = jnp.concatenate([hi, hi], axis=1)
@@ -218,14 +232,10 @@
         return acc, pltpu.roll(rolled, LANES - BLK, 1)
 
     acc, _ = lax.fori_loop(0, chunks, step, (jnp.zeros((rank, LANES), F32), cell_t))
-    pay[0:rank, :] = acc
-    pay[rank:, :] = pack(wide_gram(raw_cyc[...]))
-
-
-def pair_kernel(mine, other, pay):
-    total = mine[...] + other[...]
-    for d in range(pay.shape[0]):
-        pay[d] = total
+    gram_cyc = pack(wide_gram(raw_cyc[...]))
+    for d in range(pay.shape[0]):
+        pay[d, 0:rank, :] = acc
+        pay[d, rank:, :] = gram_cyc
 
 
 def feats_kernel(cycles_all, got, raw_cyc, unit_cell, cyc_unit, raw_out, pay):
@@ -233,7 +243,7 @@
     total = got[0]
     for d in range(1, got.shape[0]):
         total = total + got[d]
-    gram = unpack(got[0, rank:, :])
+    gram = unpack(got[0, rank:, :] + got[1, rank:, :])
     col, row = scales(gram, cycles_all)
     inv = inverse(unit_cell[...] * (gram / (col * row)))
     raw = dot(inv[:, :rank], total[:rank] / col, ((1,), (0,)), HIGHEST)
@@ -256,6 +266,7 @@
 
 
 PARAMS = pltpu.CompilerParams(vmem_limit_bytes=VMEM_LIMIT)
+SMALL = pltpu.CompilerParams(vmem_limit_bytes=8 * 1024 * 1024)
 ANY = pl.BlockSpec(memory_space=pl.ANY)
 VMEM = pl.BlockSpec(memory_space=pltpu.VMEM)
 
@@ -268,15 +279,19 @@
     c, pay = pl.pallas_call(
         contract_kernel,
         out_shape=(shape(cells, rank, cycles), shape(n_cyc * n_feat, rank + 16, LANES)),
-        in_specs=[VMEM, VMEM, VMEM, ANY],
+        in_specs=[ANY, ANY, ANY, ANY],
         out_specs=(ANY, VMEM),
         scratch_shapes=[
             pltpu.VMEM((cells, cycles, feats), F32),
             pltpu.VMEM((cells, rank, cycles), F32),
+            pltpu.VMEM(present.shape, jnp.int32),
+            pltpu.VMEM((rank, cycles), F32),
+            pltpu.VMEM((rank, feats), F32),
             pltpu.VMEM((chunks, cycles), F32),
             pltpu.VMEM((2 * rank, 2 * feats), BF16),
             pltpu.SemaphoreType.DMA((chunks,)),
             pltpu.SemaphoreType.DMA((chunks,)),
+            pltpu.SemaphoreType.DMA((3,)),
         ],
         compiler_params=PARAMS,
         name="contract",
@@ -295,12 +310,13 @@
     pay = pl.pallas_call(
         functools.partial(spread_kernel, 2 * rank),
         out_shape=shape(n_cell, 2 * rank + 8, LANES),
+        compiler_params=SMALL,
         name="spread",
     )(got)
     got = lax.all_to_all(pay, "cell", 0, 0)
     cell_unit, raw_cyc, unit_cell, pay = pl.pallas_call(
         functools.partial(cycles_kernel, float(cells * n_cell)),
-        out_shape=(shape(rank, cells), shape(rank, cycles), shape(rank, LANES), shape(rank + 8, LANES)),
+        out_shape=(shape(rank, cells), shape(rank, cycles), shape(rank, LANES), shape(n_cell * n_cyc, rank + 8, LANES)),
         in_specs=[VMEM, VMEM, VMEM, VMEM, ANY],
         out_specs=(VMEM, VMEM, VMEM, VMEM),
         scratch_shapes=[
@@ -313,18 +329,18 @@
         compiler_params=PARAMS,
         name="cycles",
     )(present, got, raw_cell, gram_feat, tensor)
-    other = lax.ppermute(pay, "cyc", [(i, n_cyc - 1 - i) for i in range(n_cyc)])
-    pay = pl.pallas_call(pair_kernel, out_shape=shape(n_cell, rank + 8, LANES), name="pair")(pay, other)
-    got = lax.all_to_all(pay, "cell", 0, 0)
+    got = lax.all_to_all(pay, ("cell", "cyc"), 0, 0)
     cyc_unit, raw_feat, pay = pl.pallas_call(
         functools.partial(feats_kernel, float(cycles * n_cyc)),
         out_shape=(shape(rank, cycles), shape(rank, feats), shape(n_feat, rank, LANES)),
+        compiler_params=SMALL,
         name="feats",
     )(got, raw_cyc, unit_cell)
     got = lax.all_to_all(pay, "feat", 0, 0)
     feat_unit = pl.pallas_call(
         functools.partial(last_kernel, float(feats * n_feat)),
         out_shape=shape(rank, feats),
+        compiler_params=SMALL,
         name="last",
     )(got, raw_feat)
     return cell_unit.T, cyc_unit.T, feat_unit.T

time: 99.3 us -> 86.4 us (0.87)
  Pallas kernels: 30.2 us -> 20.5 us
  local copies, waits for them, and re-layouts: 3.97 us -> 2.16 us
  waiting for transfers between devices: 1.19 us -> 0 us
    all_to_all x0 -> x1, blocking collectives: none -> 16 us  [shards(): got = lax.all_to_all(pay, ('cell', 'cyc'), 0, 0)]
    all_to_all x2 -> x1, blocking collectives: 32.3 us -> 17.7 us  [shards(): got = lax.all_to_all(pay, 'cell', 0, 0)]
    pallas_call x1, Pallas kernels: 4.66 us -> 1.23 us  [shards(): pl.pallas_call(functools.partial(feats_kernel, float(cycles * n_cyc)), ou...]
    pallas_call x1, Pallas kernels: 4.74 us -> 2.71 us  [shards(): pl.pallas_call(cells_kernel, out_shape=(shape(rank, cells), shape(rank, L...]
    unnamed x16 -> x8, local copies, waits for them, and re-layouts: 3.97 us -> 2.16 us
    pallas_call x1, Pallas kernels: 1.77 us -> 0.04 us  [shards(): pl.pallas_call(functools.partial(spread_kernel, 2 * rank), out_shape=shap...]
    all_to_all x2, blocking collectives: 18.7 us -> 17 us  [shards(): got = lax.all_to_all(pay, 'feat', 0, 0)]
    pallas_call x1 -> x0, Pallas kernels: 1.49 us -> none  [shards(): pl.pallas_call(pair_kernel, out_shape=shape(n_cell, rank + 8, LANES), nam...]
  transfers between devices with their start and end apart: 1 -> 0, of which waited for: 1 -> 0; matrix products, arithmetic and copies ran while one was open for 0% -> 0% of each run, Pallas kernels for 0% -> 0%
where the time goes in v2:
time: 86.4 us; the launch traced here: 85.6 us
  blocking collectives  62.2 us (72%)
  Pallas kernels  20.5 us (24%)
  local copies, waits for them, and re-layouts  2.16 us (2%)
    all_to_all x1, blocking collectives, shards(): got = lax.all_to_all(pay, 'cell', 0, 0)  17.7 us
    all_to_all x2, blocking collectives, shards(): got = lax.all_to_all(pay, 'feat', 0, 0)  17 us
    all_to_all x1, blocking collectives, shards(): got = lax.all_to_all(pay, ('cell', 'cyc'), 0, 0)  16 us
    all_to_all x1, blocking collectives, shards(): got = lax.all_to_all(pay, ('cyc', 'feat'), 0, 0)  11.5 us
    pallas_call x1, Pallas kernels, shards(): pl.pallas_call(contract_kernel, out_shape=(shape(cells, rank, cycles), sh...  8.9 us
    pallas_call x1, Pallas kernels, shards(): pl.pallas_call(functools.partial(cycles_kernel, float(cells * n_cell)), o...  7.01 us
    pallas_call x1, Pallas kernels, shards(): pl.pallas_call(cells_kernel, out_shape=(shape(rank, cells), shape(rank, L...  2.71 us
    unnamed x8, local copies, waits for them, and re-layouts  2.16 us

profile of v2, /device:TPU:0, one launch (start us, length us, event | category | flops | bytes accessed | tf_op | source)
XLA Modules:
  0.0 85.6 jit_solution(3253718529285803180)
XLA Ops:
  0.6 0.0 copy-start
  0.6 0.7 copy-done
  1.4 0.0 copy-start.1
  1.4 0.7 copy-done.1
  2.1 0.0 copy-start.2
  2.1 0.7 copy-done.2
  2.8 0.0 copy-start.3
  2.8 8.9 %contract.1 = (f32[128,32,256]{2,1,0:T(8,128)S(1)}, f32[8,48,128]{2,1,0:T(8,128)S(1)}) custom-call(s32[8,16]{1,0:T(8,128)S(1)} %copy-done.2, f32[32,256]{1,0:T(8,128)S(1)} %bitcast.5, f32[32,128]{1,0:T(8,128)S(1)} %bitcast.6, f32[128,256,128]{2,1,0:T(8,128)} %tensor.3), custom_call_target="tpu_custom_call" | custom-call | tf_op jit(solution)/shard_map/contract/pallas_call | solution.py:279
  11.7 11.5 %all_to_all.25.got = f32[8,48,128]{2,1,0:T(8,128)S(1)} all-to-all(f32[8,48,128]{2,1,0:T(8,128)S(1)} %get-tuple-element.15), channel_id=1, replica_groups=mesh['cell'=16,'cyc'=2,'feat'=4] {'cyc','feat'}, dimensions={0} | all-to-all | bytes 393216 | tf_op jit(solution)/shard_map/all_to_all | solution.py:299
  23.2 2.7 %cells.1 = (f32[32,128]{1,0:T(8,128)S(1)}, f32[32,128]{1,0:T(8,128)S(1)}, f32[4,72,128]{2,1,0:T(8,128)S(1)}) custom-call(f32[8,48,128]{2,1,0:T(8,128)S(1)} %all_to_all.25.got, f32[128,32,256]{2,1,0:T(8,128)S(1)} %get-tuple-element.16.c_in), custom_call_target="tpu_custom_call" | custom-call | tf_op jit(solution)/shard_map/cells/pallas_call | solution.py:300
  25.9 8.9 %all_to_all.26.got = f32[4,72,128]{2,1,0:T(8,128)S(1)} all-to-all(f32[4,72,128]{2,1,0:T(8,128)S(1)} %get-tuple-element.17), channel_id=1, replica_groups=mesh['cell'=16,'cyc'=2,'feat'=4] {'feat'}, dimensions={0} | all-to-all | bytes 294912 | tf_op jit(solution)/shard_map/all_to_all | solution.py:309
  34.8 17.7 %all_to_all.27.got = f32[16,72,128]{2,1,0:T(8,128)S(1)} all-to-all(f32[16,72,128]{2,1,0:T(8,128)S(1)} %spread.1), channel_id=1, replica_groups=mesh['cell'=16,'cyc'=2,'feat'=4] {'cell'}, dimensions={0} | all-to-all | bytes 1179648 | tf_op jit(solution)/shard_map/all_to_all | solution.py:316
  52.6 0.0 copy-done.3
  52.6 7.0 %cycles.1 = (f32[32,128]{1,0:T(8,128)}, f32[32,256]{1,0:T(8,128)S(1)}, f32[32,128]{1,0:T(8,128)S(1)}, f32[32,40,128]{2,1,0:T(8,128)S(1)}) custom-call(s32[8,16]{1,0:T(8,128)S(1)} %copy-done.3, f32[16,72,128]{2,1,0:T(8,128)S(1)} %all_to_all.27.got, f32[32,128]{1,0:T(8,128)S(1)} %get-tuple-element.18.raw_cell, f32[32,128]{1,0:T(8,128)S(1)} %get-tuple-element.19.gram_feat, ...), custom_call_target="tpu_custom_call" | custom-call | tf_op jit(solution)/shard_map/cycles/pallas_call | solution.py:317
  59.6 16.0 %all_to_all.28.got = f32[32,40,128]{2,1,0:T(8,128)S(1)} all-to-all(f32[32,40,128]{2,1,0:T(8,128)S(1)} %get-tuple-element.21), channel_id=1, replica_groups=mesh['cell'=16,'cyc'=2,'feat'=4] {'cell','cyc'}, dimensions={0} | all-to-all | bytes 1310720 | tf_op jit(solution)/shard_map/all_to_all | solution.py:332
  75.6 1.2 %feats.1 = (f32[32,256]{1,0:T(8,128)}, f32[32,128]{1,0:T(8,128)S(1)}, f32[4,32,128]{2,1,0:T(8,128)S(1)}) custom-call(f32[32,40,128]{2,1,0:T(8,128)S(1)} %all_to_all.28.got, f32[32,256]{1,0:T(8,128)S(1)} %get-tuple-element.22.raw_cyc, f32[32,128]{1,0:T(8,128)S(1)} %get-tuple-element.23.unit_cell), custom_call_target="tpu_custom_call" | custom-call | tf_op jit(solution)/shard_map/feats/pallas_call | solution.py:333
  76.8 8.1 %all_to_all.29.got = f32[4,32,128]{2,1,0:T(8,128)S(1)} all-to-all(f32[4,32,128]{2,1,0:T(8,128)S(1)} %get-tuple-element.25), channel_id=1, replica_groups=mesh['cell'=16,'cyc'=2,'feat'=4] {'feat'}, dimensions={0} | all-to-all | bytes 131072 | tf_op jit(solution)/shard_map/all_to_all | solution.py:339
  84.9 0.6 last.1
  (1 shorter events, 0.0 us)
Async XLA Ops:
  0.6 0.8 copy-start
  1.4 0.7 copy-start.1
  2.1 0.7 copy-start.2
  2.8 49.8 %copy-start.3 = (s32[8,16]{1,0:T(8,128)S(1)}, s32[8,16]{1,0:T(8,128)}, u32[]{:S(2)}) copy-start(s32[8,16]{1,0:T(8,128)} %present.1) | copy-start | bytes 1540

commit v3 on v2

--- a/solution.py
+++ b/solution.py
@@ -12,7 +12,6 @@
 HIGHEST = lax.Precision.HIGHEST
 F32 = jnp.float32
 BF16 = jnp.bfloat16
-VMEM_LIMIT = 48 * 1024 * 1024
 LANES = 128
 
 
@@ -84,73 +83,97 @@
     return dot(present.astype(F32), spread, ((1,), (0,)), HIGHEST)
 
 
+def tile_groups(wide):
+    wide = wide + pltpu.roll(wide, 64, 1)
+    return wide + pltpu.roll(wide, 32, 1)
+
+
+def block_diagonal(wide):
+    return jnp.concatenate([wide if g == 0 else pltpu.roll(wide, 32 * g, 1) for g in range(4)], axis=0)
+
+
+def square(rows):
+    n = rows.shape[0]
+    return rows if n == LANES else jnp.concatenate([rows, jnp.zeros((LANES - n, LANES), F32)], axis=0)
+
+
 def contract_kernel(
-    present_in, cyc_in, feat_in, tensor, c_out, pay, t_buf, c_buf, present, cyc_t, feat_t, mask, lhs, t_sem, c_sem, in_sem
+    present_in, cyc_in, feat_in, tensor, c_out, t_buf, pay,
+    present, cyc_t, feat_t, cyc4, mask, weights, part, t_sem, in_sem,
 ):
-    cells = tensor.shape[0]
-    chunks = cells // BLK
+    cells, cycles, feats = tensor.shape
     rank = cyc_t.shape[0]
+    half = cells // 2
+    piece = 8
+    ahead = 2
+    pieces = cells // piece
+    steps = pieces // 2
     small = [
         pltpu.make_async_copy(src, dst, in_sem.at[n])
-        for n, (src, dst) in enumerate(((present_in, present), (cyc_in, cyc_t), (feat_in, feat_t)))
+        for n, (src, dst) in enumerate(((feat_in, feat_t), (cyc_in, cyc_t), (present_in, present)))
     ]
 
     def fetch(n):
-        rows = pl.ds(n * BLK, BLK)
+        rows = pl.ds(n * piece, piece)
         return pltpu.make_async_copy(tensor.at[rows], t_buf.at[rows], t_sem.at[n])
-
-    def flush(n):
-        rows = pl.ds(n * BLK, BLK)
-        return pltpu.make_async_copy(c_buf.at[rows], c_out.at[rows], c_sem.at[n])
 
     for copy in small:
         copy.start()
-    for n in range(chunks):
+    for n in range(ahead):
         fetch(n).start()
+        fetch(n + steps).start()
     for copy in small:
         copy.wait()
-    mask[...] = expand_rows(present[...])
-    hi, lo = split(feat_t[...])
-    lhs[0:rank, :] = jnp.concatenate([hi, hi], axis=1)
-    lhs[rank:, :] = jnp.concatenate([lo, jnp.zeros_like(lo)], axis=1)
+    hi, lo = split(jnp.concatenate([feat_t[...]] * 4, axis=0).T)
+    hi, lo = hi.astype(F32), lo.astype(F32)
+    group = lane_iota(feats) // rank
+    for g in range(2):
+        weights[2 * g * feats : (2 * g + 1) * feats, :] = jnp.where(
+            group == 2 * g, hi, jnp.where(group == 2 * g + 1, lo, 0.0)
+        ).astype(BF16)
+        weights[(2 * g + 1) * feats : (2 * g + 2) * feats, :] = jnp.where(group == 2 * g, hi, 0.0).astype(BF16)
+    cyc4[...] = jnp.concatenate([cyc_t[...]] * 4, axis=0).T
     gram_cyc = pack(wide_gram(cyc_t[...]))
     gram_feat = pack(wide_gram(feat_t[...]))
-    lane = lane_iota(rank)
-
-    def step(n, part):
+    first = lane_iota(1) < LANES // 2
+
+    def step(n, carry):
+        @pl.when(n + ahead < steps)
+        def _():
+            fetch(n + ahead).start()
+            fetch(n + ahead + steps).start()
+
+        @pl.when(n % (BLK // piece) == 0)
+        def _():
+            one = n // (BLK // piece)
+            two = one + half // BLK
+            for b in range(cycles // BLK):
+                row = jnp.where(first, present[one, b].astype(F32), present[two, b].astype(F32))
+                mask[b * BLK : (b + 1) * BLK, :] = jnp.broadcast_to(row, (BLK, LANES))
+
         fetch(n).wait()
-        row = mask[pl.ds(n, 1), :]
-        left = lhs[...]
-        for q in range(BLK):
-            i = n * BLK + q
-            hi, lo = split(t_buf[i])
-            out = dot(left, jnp.concatenate([hi, lo], axis=1), ((1,), (1,)))
-            c = out[:rank] * row + out[rank:] * row
-            c_buf[i] = c
-            total = jnp.sum(c * cyc_t[...], axis=1, keepdims=True)
-            part = jnp.where(lane == i, total, part)
-        flush(n).start()
-        return part
-
-    part = lax.fori_loop(0, chunks, step, jnp.zeros((rank, cells), F32))
-    for d in range(pay.shape[0]):
-        pay[d, 0:rank, :] = part
+        fetch(n + steps).wait()
+        for q in range(piece):
+            p = n * piece + q
+            pair = [*split(t_buf[p]), *split(t_buf[p + half])]
+            c = dot(jnp.concatenate(pair, axis=1), weights[...], ((1,), (0,))) * mask[...]
+            c_out[p] = c
+            part[pl.ds(p, 1), :] = jnp.sum(c * cyc4[...], axis=0, keepdims=True)
+        return carry
+
+    lax.fori_loop(0, steps, step, 0, unroll=2)
+    total = part[...] + pltpu.roll(part[...], LANES - rank, 1)
+    total = jnp.where((lane_iota(half) // rank) % 2 == 0, total, 0.0)
+    total = total[:rank] + pltpu.roll(total[rank:], rank, 1)
+    for d in range(pay.shape[0]):
+        pay[d, 0:rank, :] = total
         pay[d, rank : rank + 8, :] = gram_cyc
         pay[d, rank + 8 :, :] = gram_feat
-    for n in range(chunks):
-        flush(n).wait()
-
-
-def cells_kernel(got, c_in, raw_out, gram_feat_out, pay, c_buf, c_sem):
-    cells, rank = c_in.shape[0], c_in.shape[1]
-    chunks = cells // BLK
-
-    def fetch(n):
-        rows = pl.ds(n * BLK, BLK)
-        return pltpu.make_async_copy(c_in.at[rows], c_buf.at[rows], c_sem.at[n])
-
-    for n in range(chunks):
-        fetch(n).start()
+
+
+def cells_kernel(got, c_in, raw_out, gram_feat_out, pay, pairs):
+    half, cycles = c_in.shape[0], c_in.shape[1]
+    rank = raw_out.shape[0]
     part = got[0, 0:rank, :]
     for d in range(1, 8):
         part = part + got[d, 0:rank, :]
@@ -161,22 +184,35 @@
     gram_feat = unpack(gram_feat)
     gram_feat_out[...] = gram_feat
     inv = inverse(gram_cyc * gram_feat)
-    raw = dot(inv[:, :rank], part, ((1,), (0,)), HIGHEST)
+    raw = dot(part, block_diagonal(inv), ((1,), (0,)), HIGHEST)
     raw_out[...] = raw
-    gram = pack(wide_gram(raw))
-
-    def step(n, carry):
-        fetch(n).wait()
-        total, rolled = carry
-        for q in range(BLK):
-            total = total + c_buf[n * BLK + q] * rolled[:, q : q + 1]
-        return total, pltpu.roll(rolled, LANES - BLK, 1)
-
-    total, _ = lax.fori_loop(0, chunks, step, (jnp.zeros((rank, c_in.shape[2]), F32), raw))
-    for d in range(pay.shape[0]):
-        pay[d, 0:rank, :] = total[:, :LANES]
-        pay[d, rank : 2 * rank, :] = total[:, LANES:]
-        pay[d, 2 * rank :, :] = gram
+    even = (lane_iota(rank) // rank) % 2 == 0
+    one, two = jnp.where(even, raw, 0.0), jnp.where(even, 0.0, raw)
+    pairs[0:rank, :] = one + pltpu.roll(one, rank, 1)
+    pairs[rank:, :] = two + pltpu.roll(two, LANES - rank, 1)
+    full = dot(raw, raw, ((0,), (0,)), HIGHEST)
+    gram = full[:rank]
+    for g in range(1, 4):
+        gram = gram + pltpu.roll(full[g * rank : (g + 1) * rank], LANES - g * rank, 1)
+    gram = pack(jnp.where(lane_iota(rank) < rank, gram, 0.0))
+    rows = cycles // 4
+    group = lane_iota(rows) // rank
+    packed = jnp.zeros((rows, LANES), F32)
+    for g in range(4):
+
+        def step(n, acc, g=g):
+            for q in range(16):
+                p = n * 16 + q
+                acc = acc + c_in[p, g * rows : (g + 1) * rows, :] * pairs[pl.ds(p, 1), :]
+            return acc
+
+        acc = lax.fori_loop(0, half // 16, step, jnp.zeros((rows, LANES), F32))
+        acc = acc + pltpu.roll(acc, 64, 1)
+        acc = acc + pltpu.roll(acc, 32, 1)
+        packed = jnp.where(group == g, acc, packed)
+    for d in range(pay.shape[0]):
+        pay[d, 0:rows, :] = packed
+        pay[d, rows:, :] = gram
 
 
 def spread_kernel(rows, got, pay):
@@ -190,18 +226,11 @@
 
 def cycles_kernel(
     cells_all, present, got, raw_cell, gram_feat, tensor,
-    cell_unit, raw_cyc_out, unit_out, pay, t_buf, mask, raw_cyc, wide, t_sem,
+    cell_unit, raw_cyc_out, unit_out, pay, mask, raw_cyc, wide,
 ):
     cells = tensor.shape[0]
     chunks = cells // BLK
     rank = raw_cell.shape[0]
-
-    def fetch(n):
-        rows = pl.ds(n * BLK, BLK)
-        return pltpu.make_async_copy(tensor.at[rows], t_buf.at[rows], t_sem.at[n])
-
-    for n in range(chunks):
-        fetch(n).start()
     mask[...] = expand_rows(present[...])
     total = got[0]
     for d in range(1, got.shape[0]):
@@ -211,20 +240,25 @@
     unit = gram / (col * row)
     unit_out[...] = unit
     inv = inverse(unit * gram_feat[...])
+    scale = tile_groups(jnp.where(lane_iota(1) < rank, row, 0.0))
+    raw = square(dot(total[: 2 * rank] / scale, block_diagonal(inv), ((1,), (0,)), HIGHEST)).T
     for h in range(2):
-        half = total[h * rank : (h + 1) * rank] / col
-        raw_cyc[:, h * LANES : (h + 1) * LANES] = dot(inv[:, :rank], half, ((1,), (0,)), HIGHEST)
+        raw_cyc[:, h * LANES : (h + 1) * LANES] = raw[2 * h * rank : (2 * h + 1) * rank] + pltpu.roll(
+            raw[(2 * h + 1) * rank : (2 * h + 2) * rank], LANES // 2, 1
+        )
     raw_cyc_out[...] = raw_cyc[...]
-    cell_t = raw_cell[...] / col
+    unit_cell = square(raw_cell[...] / scale).T
+    cell_t = unit_cell[:rank]
+    for g in range(1, 4):
+        cell_t = cell_t + pltpu.roll(unit_cell[g * rank : (g + 1) * rank], g * rank, 1)
     cell_unit[...] = cell_t
 
     def step(n, carry):
         acc, rolled = carry
-        fetch(n).wait()
         hi, lo = split(raw_cyc[...] * mask[pl.ds(n, 1), :])
         left = jnp.concatenate([hi, lo], axis=0)
         for q in range(BLK):
-            hi, lo = split(t_buf[n * BLK + q])
+            hi, lo = split(tensor[n * BLK + q])
             wide[q] = dot(left, jnp.concatenate([hi, lo], axis=1), ((1,), (0,)))
         for q in range(BLK):
             w = wide[q, :rank, :LANES] + (wide[q, :rank, LANES:] + wide[q, rank:, :LANES])
@@ -265,7 +299,6 @@
     return jax.ShapeDtypeStruct(dims, F32)
 
 
-PARAMS = pltpu.CompilerParams(vmem_limit_bytes=VMEM_LIMIT)
 SMALL = pltpu.CompilerParams(vmem_limit_bytes=8 * 1024 * 1024)
 ANY = pl.BlockSpec(memory_space=pl.ANY)
 VMEM = pl.BlockSpec(memory_space=pltpu.VMEM)
@@ -276,34 +309,38 @@
     rank = cyc_factor.shape[1]
     chunks = cells // BLK
     n_cell, n_cyc, n_feat = (lax.axis_size(a) for a in ("cell", "cyc", "feat"))
-    c, pay = pl.pallas_call(
+    far = [pltpu.with_memory_space_constraint(x, pltpu.HBM) for x in (present, cyc_factor.T, feat_factor.T, tensor)]
+    c, kept, pay = pl.pallas_call(
         contract_kernel,
-        out_shape=(shape(cells, rank, cycles), shape(n_cyc * n_feat, rank + 16, LANES)),
+        out_shape=(
+            pltpu.VMEM((cells // 2, cycles, LANES), F32),
+            pltpu.VMEM((cells, cycles, feats), F32),
+            shape(n_cyc * n_feat, rank + 16, LANES),
+        ),
         in_specs=[ANY, ANY, ANY, ANY],
-        out_specs=(ANY, VMEM),
+        out_specs=(VMEM, VMEM, VMEM),
         scratch_shapes=[
-            pltpu.VMEM((cells, cycles, feats), F32),
-            pltpu.VMEM((cells, rank, cycles), F32),
-            pltpu.VMEM(present.shape, jnp.int32),
+            pltpu.SMEM(present.shape, jnp.int32),
             pltpu.VMEM((rank, cycles), F32),
             pltpu.VMEM((rank, feats), F32),
-            pltpu.VMEM((chunks, cycles), F32),
-            pltpu.VMEM((2 * rank, 2 * feats), BF16),
-            pltpu.SemaphoreType.DMA((chunks,)),
-            pltpu.SemaphoreType.DMA((chunks,)),
+            pltpu.VMEM((cycles, LANES), F32),
+            pltpu.VMEM((cycles, LANES), F32),
+            pltpu.VMEM((4 * feats, LANES), BF16),
+            pltpu.VMEM((cells // 2, LANES), F32),
+            pltpu.SemaphoreType.DMA((cells // 8,)),
             pltpu.SemaphoreType.DMA((3,)),
         ],
-        compiler_params=PARAMS,
+        compiler_params=SMALL,
         name="contract",
-    )(present, cyc_factor.T, feat_factor.T, tensor)
+    )(*far)
     got = lax.all_to_all(pay, ("cyc", "feat"), 0, 0)
     raw_cell, gram_feat, pay = pl.pallas_call(
         cells_kernel,
-        out_shape=(shape(rank, cells), shape(rank, LANES), shape(n_feat, 2 * rank + 8, LANES)),
-        in_specs=[VMEM, ANY],
+        out_shape=(shape(rank, LANES), shape(rank, LANES), shape(n_feat, 2 * rank + 8, LANES)),
+        in_specs=[VMEM, VMEM],
         out_specs=(VMEM, VMEM, VMEM),
-        scratch_shapes=[pltpu.VMEM((cells, rank, cycles), F32), pltpu.SemaphoreType.DMA((chunks,))],
-        compiler_params=PARAMS,
+        scratch_shapes=[pltpu.VMEM((cells // 2, LANES), F32)],
+        compiler_params=SMALL,
         name="cells",
     )(got, c)
     got = lax.all_to_all(pay, "feat", 0, 0)
@@ -317,18 +354,16 @@
     cell_unit, raw_cyc, unit_cell, pay = pl.pallas_call(
         functools.partial(cycles_kernel, float(cells * n_cell)),
         out_shape=(shape(rank, cells), shape(rank, cycles), shape(rank, LANES), shape(n_cell * n_cyc, rank + 8, LANES)),
-        in_specs=[VMEM, VMEM, VMEM, VMEM, ANY],
+        in_specs=[VMEM, VMEM, VMEM, VMEM, VMEM],
         out_specs=(VMEM, VMEM, VMEM, VMEM),
         scratch_shapes=[
-            pltpu.VMEM((cells, cycles, feats), F32),
             pltpu.VMEM((chunks, cycles), F32),
             pltpu.VMEM((rank, cycles), F32),
             pltpu.VMEM((BLK, 2 * rank, 2 * feats), F32),
-            pltpu.SemaphoreType.DMA((chunks,)),
         ],
-        compiler_params=PARAMS,
+        compiler_params=SMALL,
         name="cycles",
-    )(present, got, raw_cell, gram_feat, tensor)
+    )(present, got, raw_cell, gram_feat, kept)
     got = lax.all_to_all(pay, ("cell", "cyc"), 0, 0)
     cyc_unit, raw_feat, pay = pl.pallas_call(
         functools.partial(feats_kernel, float(cycles * n_cyc)),

time: 86.4 us -> 82.1 us (0.950)
  local copies, waits for them, and re-layouts: 2.16 us -> 0.01 us
  Pallas kernels: 20.5 us -> 18.5 us
    unnamed x8 -> x2, local copies, waits for them, and re-layouts: 2.16 us -> 0.01 us
    pallas_call x1, Pallas kernels: 7.01 us -> 5.7 us  [shards(): pl.pallas_call(functools.partial(cycles_kernel, float(cells * n_cell)), o...]
where the time goes in v3:
time: 82.1 us; the launch traced here: 81.3 us
  blocking collectives  62.2 us (76%)
  Pallas kernels  18.5 us (23%)
    all_to_all x1, blocking collectives, shards(): got = lax.all_to_all(pay, 'cell', 0, 0)  17.7 us
    all_to_all x2, blocking collectives, shards(): got = lax.all_to_all(pay, 'feat', 0, 0)  17 us
    all_to_all x1, blocking collectives, shards(): got = lax.all_to_all(pay, ('cell', 'cyc'), 0, 0)  16 us
    all_to_all x1, blocking collectives, shards(): got = lax.all_to_all(pay, ('cyc', 'feat'), 0, 0)  11.5 us
    pallas_call x1, Pallas kernels, shards(): pl.pallas_call(contract_kernel, out_shape=(pltpu.VMEM((cells // 2, cycles...  8.3 us
    pallas_call x1, Pallas kernels, shards(): pl.pallas_call(functools.partial(cycles_kernel, float(cells * n_cell)), o...  5.7 us
    pallas_call x1, Pallas kernels, shards(): pl.pallas_call(cells_kernel, out_shape=(shape(rank, LANES), shape(rank, L...  2.58 us

profile of v3, /device:TPU:0, one launch (start us, length us, event | category | flops | bytes accessed | tf_op | source)
XLA Modules:
  0.0 81.3 jit_solution(8726028826584160136)
XLA Ops:
  0.6 0.0 copy-start
  0.6 8.3 %contract.1 = (f32[64,256,128]{2,1,0:T(8,128)S(1)}, f32[128,256,128]{2,1,0:T(8,128)S(1)}, f32[8,48,128]{2,1,0:T(8,128)S(1)}) custom-call(s32[8,16]{1,0:T(8,128)} %present.1, f32[32,256]{1,0:T(8,128)} %bitcast.5, f32[32,128]{1,0:T(8,128)} %bitcast.7, f32[128,256,128]{2,1,0:T(8,128)} %tensor.1), custom_call_target="tpu_custom_call" | custom-call | tf_op jit(solution)/shard_map/contract/pallas_call | solution.py:313
  8.9 11.5 %all_to_all.25.got = f32[8,48,128]{2,1,0:T(8,128)S(1)} all-to-all(f32[8,48,128]{2,1,0:T(8,128)S(1)} %get-tuple-element.16), channel_id=1, replica_groups=mesh['cell'=16,'cyc'=2,'feat'=4] {'cyc','feat'}, dimensions={0} | all-to-all | bytes 393216 | tf_op jit(solution)/shard_map/all_to_all | solution.py:336
  20.4 2.6 %cells.1 = (f32[32,128]{1,0:T(8,128)S(1)}, f32[32,128]{1,0:T(8,128)S(1)}, f32[4,72,128]{2,1,0:T(8,128)S(1)}) custom-call(f32[8,48,128]{2,1,0:T(8,128)S(1)} %all_to_all.25.got, f32[64,256,128]{2,1,0:T(8,128)S(1)} %get-tuple-element.17.c_in), custom_call_target="tpu_custom_call" | custom-call | tf_op jit(solution)/shard_map/cells/pallas_call | solution.py:337
  23.0 8.9 %all_to_all.26.got = f32[4,72,128]{2,1,0:T(8,128)S(1)} all-to-all(f32[4,72,128]{2,1,0:T(8,128)S(1)} %get-tuple-element.18), channel_id=1, replica_groups=mesh['cell'=16,'cyc'=2,'feat'=4] {'feat'}, dimensions={0} | all-to-all | bytes 294912 | tf_op jit(solution)/shard_map/all_to_all | solution.py:346
  31.9 17.7 %all_to_all.27.got = f32[16,72,128]{2,1,0:T(8,128)S(1)} all-to-all(f32[16,72,128]{2,1,0:T(8,128)S(1)} %spread.1), channel_id=1, replica_groups=mesh['cell'=16,'cyc'=2,'feat'=4] {'cell'}, dimensions={0} | all-to-all | bytes 1179648 | tf_op jit(solution)/shard_map/all_to_all | solution.py:353
  49.7 0.0 copy-done
  49.7 5.7 %cycles.1 = (f32[32,128]{1,0:T(8,128)}, f32[32,256]{1,0:T(8,128)S(1)}, f32[32,128]{1,0:T(8,128)S(1)}, f32[32,40,128]{2,1,0:T(8,128)S(1)}) custom-call(s32[8,16]{1,0:T(8,128)S(1)} %copy-done, f32[16,72,128]{2,1,0:T(8,128)S(1)} %all_to_all.27.got, f32[32,128]{1,0:T(8,128)S(1)} %get-tuple-element.19.raw_cell, f32[32,128]{1,0:T(8,128)S(1)} %get-tuple-element.20.gram_feat, ...), custom_call_target="tpu_custom_call" | custom-call | tf_op jit(solution)/shard_map/cycles/pallas_call | solution.py:354
  55.4 16.0 %all_to_all.28.got = f32[32,40,128]{2,1,0:T(8,128)S(1)} all-to-all(f32[32,40,128]{2,1,0:T(8,128)S(1)} %get-tuple-element.23), channel_id=1, replica_groups=mesh['cell'=16,'cyc'=2,'feat'=4] {'cell','cyc'}, dimensions={0} | all-to-all | bytes 1310720 | tf_op jit(solution)/shard_map/all_to_all | solution.py:367
  71.4 1.2 %feats.1 = (f32[32,256]{1,0:T(8,128)}, f32[32,128]{1,0:T(8,128)S(1)}, f32[4,32,128]{2,1,0:T(8,128)S(1)}) custom-call(f32[32,40,128]{2,1,0:T(8,128)S(1)} %all_to_all.28.got, f32[32,256]{1,0:T(8,128)S(1)} %get-tuple-element.24.raw_cyc, f32[32,128]{1,0:T(8,128)S(1)} %get-tuple-element.25.unit_cell), custom_call_target="tpu_custom_call" | custom-call | tf_op jit(solution)/shard_map/feats/pallas_call | solution.py:368
  72.6 8.1 %all_to_all.29.got = f32[4,32,128]{2,1,0:T(8,128)S(1)} all-to-all(f32[4,32,128]{2,1,0:T(8,128)S(1)} %get-tuple-element.27), channel_id=1, replica_groups=mesh['cell'=16,'cyc'=2,'feat'=4] {'feat'}, dimensions={0} | all-to-all | bytes 131072 | tf_op jit(solution)/shard_map/all_to_all | solution.py:374
  80.7 0.6 last.1
  (1 shorter events, 0.0 us)
Async XLA Ops:
  0.6 49.0 %copy-start = (s32[8,16]{1,0:T(8,128)S(1)}, s32[8,16]{1,0:T(8,128)}, u32[]{:S(2)}) copy-start(s32[8,16]{1,0:T(8,128)} %present.1) | copy-start | bytes 1540

commit v4 on v3

--- a/solution.py
+++ b/solution.py
@@ -104,24 +104,26 @@
     cells, cycles, feats = tensor.shape
     rank = cyc_t.shape[0]
     half = cells // 2
-    piece = 8
+    sizes = (8,) * (half // 8)
+    starts = [sum(sizes[:n]) for n in range(len(sizes))]
     ahead = 2
-    pieces = cells // piece
-    steps = pieces // 2
     small = [
         pltpu.make_async_copy(src, dst, in_sem.at[n])
         for n, (src, dst) in enumerate(((feat_in, feat_t), (cyc_in, cyc_t), (present_in, present)))
     ]
 
     def fetch(n):
-        rows = pl.ds(n * piece, piece)
-        return pltpu.make_async_copy(tensor.at[rows], t_buf.at[rows], t_sem.at[n])
+        both = []
+        for h in range(2):
+            rows = pl.ds(starts[n] + h * half, sizes[n])
+            both.append(pltpu.make_async_copy(tensor.at[rows], t_buf.at[rows], t_sem.at[2 * n + h]))
+        return both
 
     for copy in small:
         copy.start()
     for n in range(ahead):
-        fetch(n).start()
-        fetch(n + steps).start()
+        for copy in fetch(n):
+            copy.start()
     for copy in small:
         copy.wait()
     hi, lo = split(jnp.concatenate([feat_t[...]] * 4, axis=0).T)
@@ -137,31 +139,24 @@
     gram_feat = pack(wide_gram(feat_t[...]))
     first = lane_iota(1) < LANES // 2
 
-    def step(n, carry):
-        @pl.when(n + ahead < steps)
-        def _():
-            fetch(n + ahead).start()
-            fetch(n + ahead + steps).start()
-
-        @pl.when(n % (BLK // piece) == 0)
-        def _():
-            one = n // (BLK // piece)
+    for n in range(len(sizes)):
+        if n + ahead < len(sizes):
+            for copy in fetch(n + ahead):
+                copy.start()
+        if starts[n] % BLK == 0:
+            one = starts[n] // BLK
             two = one + half // BLK
             for b in range(cycles // BLK):
                 row = jnp.where(first, present[one, b].astype(F32), present[two, b].astype(F32))
                 mask[b * BLK : (b + 1) * BLK, :] = jnp.broadcast_to(row, (BLK, LANES))
-
-        fetch(n).wait()
-        fetch(n + steps).wait()
-        for q in range(piece):
-            p = n * piece + q
+        for copy in fetch(n):
+            copy.wait()
+        for p in range(starts[n], starts[n] + sizes[n]):
             pair = [*split(t_buf[p]), *split(t_buf[p + half])]
             c = dot(jnp.concatenate(pair, axis=1), weights[...], ((1,), (0,))) * mask[...]
             c_out[p] = c
-            part[pl.ds(p, 1), :] = jnp.sum(c * cyc4[...], axis=0, keepdims=True)
-        return carry
-
-    lax.fori_loop(0, steps, step, 0, unroll=2)
+            part[p : p + 1, :] = jnp.sum(c * cyc4[...], axis=0, keepdims=True)
+
     total = part[...] + pltpu.roll(part[...], LANES - rank, 1)
     total = jnp.where((lane_iota(half) // rank) % 2 == 0, total, 0.0)
     total = total[:rank] + pltpu.roll(total[rank:], rank, 1)
@@ -226,7 +221,7 @@
 
 def cycles_kernel(
     cells_all, present, got, raw_cell, gram_feat, tensor,
-    cell_unit, raw_cyc_out, unit_out, pay, mask, raw_cyc, wide,
+    cell_unit, raw_cyc_out, unit_out, pay, mask, raw_cyc, cell_buf, wide, sem,
 ):
     cells = tensor.shape[0]
     chunks = cells // BLK
@@ -251,7 +246,9 @@
     cell_t = unit_cell[:rank]
     for g in range(1, 4):
         cell_t = cell_t + pltpu.roll(unit_cell[g * rank : (g + 1) * rank], g * rank, 1)
-    cell_unit[...] = cell_t
+    cell_buf[...] = cell_t
+    leave = pltpu.make_async_copy(cell_buf, cell_unit, sem.at[0])
+    leave.start()
 
     def step(n, carry):
         acc, rolled = carry
@@ -266,26 +263,33 @@
         return acc, pltpu.roll(rolled, LANES - BLK, 1)
 
     acc, _ = lax.fori_loop(0, chunks, step, (jnp.zeros((rank, LANES), F32), cell_t))
-    gram_cyc = pack(wide_gram(raw_cyc[...]))
+    pay[0:rank, :] = acc
+    pay[rank:, :] = pack(wide_gram(raw_cyc[...]))
+    leave.wait()
+
+
+def pair_kernel(mine, other, pay):
     for d in range(pay.shape[0]):
-        pay[d, 0:rank, :] = acc
-        pay[d, rank:, :] = gram_cyc
-
-
-def feats_kernel(cycles_all, got, raw_cyc, unit_cell, cyc_unit, raw_out, pay):
+        pay[d] = mine[...] + other[...]
+
+
+def feats_kernel(cycles_all, got, raw_cyc, unit_cell, cyc_unit, raw_out, pay, cyc_buf, sem):
     rank = raw_cyc.shape[0]
     total = got[0]
     for d in range(1, got.shape[0]):
         total = total + got[d]
-    gram = unpack(got[0, rank:, :] + got[1, rank:, :])
+    gram = unpack(got[0, rank:, :])
     col, row = scales(gram, cycles_all)
+    cyc_buf[...] = raw_cyc[...] / col
+    leave = pltpu.make_async_copy(cyc_buf, cyc_unit, sem.at[0])
+    leave.start()
     inv = inverse(unit_cell[...] * (gram / (col * row)))
     raw = dot(inv[:, :rank], total[:rank] / col, ((1,), (0,)), HIGHEST)
     raw_out[...] = raw
     square = jnp.broadcast_to(jnp.sum(raw * raw, axis=1, keepdims=True), (rank, LANES))
     for d in range(pay.shape[0]):
         pay[d] = square
-    cyc_unit[...] = raw_cyc[...] / col
+    leave.wait()
 
 
 def last_kernel(feats_all, got, raw, feat_unit):
@@ -327,7 +331,7 @@
             pltpu.VMEM((cycles, LANES), F32),
             pltpu.VMEM((4 * feats, LANES), BF16),
             pltpu.VMEM((cells // 2, LANES), F32),
-            pltpu.SemaphoreType.DMA((cells // 8,)),
+            pltpu.SemaphoreType.DMA((cells // 4,)),
             pltpu.SemaphoreType.DMA((3,)),
         ],
         compiler_params=SMALL,
@@ -353,21 +357,33 @@
     got = lax.all_to_all(pay, "cell", 0, 0)
     cell_unit, raw_cyc, unit_cell, pay = pl.pallas_call(
         functools.partial(cycles_kernel, float(cells * n_cell)),
-        out_shape=(shape(rank, cells), shape(rank, cycles), shape(rank, LANES), shape(n_cell * n_cyc, rank + 8, LANES)),
+        out_shape=(pltpu.HBM((rank, cells), F32), shape(rank, cycles), shape(rank, LANES), shape(rank + 8, LANES)),
         in_specs=[VMEM, VMEM, VMEM, VMEM, VMEM],
-        out_specs=(VMEM, VMEM, VMEM, VMEM),
+        out_specs=(ANY, VMEM, VMEM, VMEM),
         scratch_shapes=[
             pltpu.VMEM((chunks, cycles), F32),
             pltpu.VMEM((rank, cycles), F32),
+            pltpu.VMEM((rank, cells), F32),
             pltpu.VMEM((BLK, 2 * rank, 2 * feats), F32),
+            pltpu.SemaphoreType.DMA((1,)),
         ],
         compiler_params=SMALL,
         name="cycles",
     )(present, got, raw_cell, gram_feat, kept)
-    got = lax.all_to_all(pay, ("cell", "cyc"), 0, 0)
+    other = lax.ppermute(pay, "cyc", [(i, n_cyc - 1 - i) for i in range(n_cyc)])
+    pay = pl.pallas_call(
+        pair_kernel,
+        out_shape=shape(n_cell, rank + 8, LANES),
+        compiler_params=SMALL,
+        name="pair",
+    )(pay, other)
+    got = lax.all_to_all(pay, "cell", 0, 0)
     cyc_unit, raw_feat, pay = pl.pallas_call(
         functools.partial(feats_kernel, float(cycles * n_cyc)),
-        out_shape=(shape(rank, cycles), shape(rank, feats), shape(n_feat, rank, LANES)),
+        out_shape=(pltpu.HBM((rank, cycles), F32), shape(rank, feats), shape(n_feat, rank, LANES)),
+        in_specs=[VMEM, VMEM, VMEM],
+        out_specs=(ANY, VMEM, VMEM),
+        scratch_shapes=[pltpu.VMEM((rank, cycles), F32), pltpu.SemaphoreType.DMA((1,))],
         compiler_params=SMALL,
         name="feats",
     )(got, raw_cyc, unit_cell)

time: 82.1 us -> 79.4 us (0.967)
  blocking collectives: 62.2 us -> 58.9 us
  waiting for transfers between devices: 0 us -> 1.18 us
    all_to_all x1 -> x0, blocking collectives: 16 us -> none  [shards(): got = lax.all_to_all(pay, ('cell', 'cyc'), 0, 0)]
    all_to_all x1 -> x2, blocking collectives: 17.7 us -> 30.5 us  [shards(): got = lax.all_to_all(pay, 'cell', 0, 0)]
    ppermute x0 -> x1, waiting for transfers between devices: none -> 1.18 us  [shards(): other = lax.ppermute(pay, 'cyc', [(i, n_cyc - 1 - i) for i in range(n_cyc)])]
  transfers between devices with their start and end apart: 0 -> 1, of which waited for: 0 -> 1; matrix products, arithmetic and copies ran while one was open for 0% -> 0% of each run, Pallas kernels for 0% -> 0%
where the time goes in v4:
time: 79.4 us; the launch traced here: 79 us
  blocking collectives  58.9 us (74%)
  Pallas kernels  18.2 us (23%)
  waiting for transfers between devices  1.18 us (1%)
    all_to_all x2, blocking collectives, shards(): got = lax.all_to_all(pay, 'cell', 0, 0)  30.5 us
    all_to_all x2, blocking collectives, shards(): got = lax.all_to_all(pay, 'feat', 0, 0)  17 us
    all_to_all x1, blocking collectives, shards(): got = lax.all_to_all(pay, ('cyc', 'feat'), 0, 0)  11.5 us
    pallas_call x1, Pallas kernels, shards(): pl.pallas_call(contract_kernel, out_shape=(pltpu.VMEM((cells // 2, cycles...  8.21 us
    pallas_call x1, Pallas kernels, shards(): pl.pallas_call(functools.partial(cycles_kernel, float(cells * n_cell)), o...  5.47 us
    pallas_call x1, Pallas kernels, shards(): pl.pallas_call(cells_kernel, out_shape=(shape(rank, LANES), shape(rank, L...  2.58 us
  transfers between devices with their start and end apart: 1, of which 1 were waited for; matrix products, arithmetic and copies ran while one was open for 0% of the time, Pallas kernels for 0%

profile of v4, /device:TPU:0, one launch (start us, length us, event | category | flops | bytes accessed | tf_op | source)
XLA Modules:
  0.0 79.0 jit_solution(15178777919428554856)
XLA Ops:
  0.6 0.0 copy-start
  0.6 8.2 %contract.1 = (f32[64,256,128]{2,1,0:T(8,128)S(1)}, f32[128,256,128]{2,1,0:T(8,128)S(1)}, f32[8,48,128]{2,1,0:T(8,128)S(1)}) custom-call(s32[8,16]{1,0:T(8,128)} %present.1, f32[32,256]{1,0:T(8,128)} %bitcast.5, f32[32,128]{1,0:T(8,128)} %bitcast.7, f32[128,256,128]{2,1,0:T(8,128)} %tensor.1), custom_call_target="tpu_custom_call" | custom-call | tf_op jit(solution)/shard_map/contract/pallas_call | solution.py:317
  8.9 11.5 %all_to_all.25.got = f32[8,48,128]{2,1,0:T(8,128)S(1)} all-to-all(f32[8,48,128]{2,1,0:T(8,128)S(1)} %get-tuple-element.16), channel_id=1, replica_groups=mesh['cell'=16,'cyc'=2,'feat'=4] {'cyc','feat'}, dimensions={0} | all-to-all | bytes 393216 | tf_op jit(solution)/shard_map/all_to_all | solution.py:340
  20.3 2.6 %cells.1 = (f32[32,128]{1,0:T(8,128)S(1)}, f32[32,128]{1,0:T(8,128)S(1)}, f32[4,72,128]{2,1,0:T(8,128)S(1)}) custom-call(f32[8,48,128]{2,1,0:T(8,128)S(1)} %all_to_all.25.got, f32[64,256,128]{2,1,0:T(8,128)S(1)} %get-tuple-element.17.c_in), custom_call_target="tpu_custom_call" | custom-call | tf_op jit(solution)/shard_map/cells/pallas_call | solution.py:341
  22.9 8.9 %all_to_all.26.got = f32[4,72,128]{2,1,0:T(8,128)S(1)} all-to-all(f32[4,72,128]{2,1,0:T(8,128)S(1)} %get-tuple-element.18), channel_id=1, replica_groups=mesh['cell'=16,'cyc'=2,'feat'=4] {'feat'}, dimensions={0} | all-to-all | bytes 294912 | tf_op jit(solution)/shard_map/all_to_all | solution.py:350
  31.8 17.7 %all_to_all.27.got = f32[16,72,128]{2,1,0:T(8,128)S(1)} all-to-all(f32[16,72,128]{2,1,0:T(8,128)S(1)} %spread.1), channel_id=1, replica_groups=mesh['cell'=16,'cyc'=2,'feat'=4] {'cell'}, dimensions={0} | all-to-all | bytes 1179648 | tf_op jit(solution)/shard_map/all_to_all | solution.py:357
  49.6 0.0 copy-done
  49.6 5.5 %cycles.1 = (f32[32,128]{1,0:T(8,128)}, f32[32,256]{1,0:T(8,128)S(1)}, f32[32,128]{1,0:T(8,128)S(1)}, f32[40,128]{1,0:T(8,128)S(1)}) custom-call(s32[8,16]{1,0:T(8,128)S(1)} %copy-done, f32[16,72,128]{2,1,0:T(8,128)S(1)} %all_to_all.27.got, f32[32,128]{1,0:T(8,128)S(1)} %get-tuple-element.19.raw_cell, f32[32,128]{1,0:T(8,128)S(1)} %get-tuple-element.20.gram_feat, ...), custom_call_target="tpu_custom_call" | custom-call | tf_op jit(solution)/shard_map/cycles/pallas_call | solution.py:358
  55.0 0.1 collective-permute-start
  55.1 1.2 %collective-permute-done.other = f32[40,128]{1,0:T(8,128)S(1)} collective-permute-done((f32[40,128]{1,0:T(8,128)S(1)}, f32[40,128]{1,0:T(8,128)S(1)}, u32[]{:S(2)}, u32[]{:S(2)}) %collective-permute-start) | collective-permute-done | bytes 20512 | tf_op jit(solution)/shard_map/ppermute | solution.py:373
  56.3 12.7 %all_to_all.28.got = f32[16,40,128]{2,1,0:T(8,128)S(1)} all-to-all(f32[16,40,128]{2,1,0:T(8,128)S(1)} %pair.1), channel_id=1, replica_groups=mesh['cell'=16,'cyc'=2,'feat'=4] {'cell'}, dimensions={0} | all-to-all | bytes 655360 | tf_op jit(solution)/shard_map/all_to_all | solution.py:380
  69.1 1.2 %feats.1 = (f32[32,256]{1,0:T(8,128)}, f32[32,128]{1,0:T(8,128)S(1)}, f32[4,32,128]{2,1,0:T(8,128)S(1)}) custom-call(f32[16,40,128]{2,1,0:T(8,128)S(1)} %all_to_all.28.got, f32[32,256]{1,0:T(8,128)S(1)} %get-tuple-element.24.raw_cyc, f32[32,128]{1,0:T(8,128)S(1)} %get-tuple-element.25.unit_cell), custom_call_target="tpu_custom_call" | custom-call | tf_op jit(solution)/shard_map/feats/pallas_call | solution.py:381
  70.3 8.1 %all_to_all.29.got = f32[4,32,128]{2,1,0:T(8,128)S(1)} all-to-all(f32[4,32,128]{2,1,0:T(8,128)S(1)} %get-tuple-element.27), channel_id=1, replica_groups=mesh['cell'=16,'cyc'=2,'feat'=4] {'feat'}, dimensions={0} | all-to-all | bytes 131072 | tf_op jit(solution)/shard_map/all_to_all | solution.py:390
  78.4 0.6 last.1
  (2 shorter events, 0.1 us)
Async XLA Ops:
  0.6 48.9 %copy-start = (s32[8,16]{1,0:T(8,128)S(1)}, s32[8,16]{1,0:T(8,128)}, u32[]{:S(2)}) copy-start(s32[8,16]{1,0:T(8,128)} %present.1) | copy-start | bytes 1540
  55.0 1.3 %collective-permute-start = (f32[40,128]{1,0:T(8,128)S(1)}, f32[40,128]{1,0:T(8,128)S(1)}, u32[]{:S(2)}, u32[]{:S(2)}) collective-permute-start(f32[40,128]{1,0:T(8,128)S(1)} %get-tuple-element.23.mine), channel_id=1, source_target_pairs={{0,4},{4,0},{1,5},{5,1},{2,6},{6,2},{3,7},{7,3},{8,12},{12,8},{9,1... | collective-permute-start | bytes 61448 | tf_op jit(solution)/shard_map/ppermute | solution.py:373

commit v5 on v4

--- a/solution.py
+++ b/solution.py
@@ -201,7 +201,7 @@
                 acc = acc + c_in[p, g * rows : (g + 1) * rows, :] * pairs[pl.ds(p, 1), :]
             return acc
 
-        acc = lax.fori_loop(0, half // 16, step, jnp.zeros((rows, LANES), F32))
+        acc = lax.fori_loop(0, half // 16, step, jnp.zeros((rows, LANES), F32), unroll=True)
         acc = acc + pltpu.roll(acc, 64, 1)
         acc = acc + pltpu.roll(acc, 32, 1)
         packed = jnp.where(group == g, acc, packed)
@@ -262,7 +262,7 @@
             acc = acc + w * rolled[:, q : q + 1]
         return acc, pltpu.roll(rolled, LANES - BLK, 1)
 
-    acc, _ = lax.fori_loop(0, chunks, step, (jnp.zeros((rank, LANES), F32), cell_t))
+    acc, _ = lax.fori_loop(0, chunks, step, (jnp.zeros((rank, LANES), F32), cell_t), unroll=4)
     pay[0:rank, :] = acc
     pay[rank:, :] = pack(wide_gram(raw_cyc[...]))
     leave.wait()

time: 79.4 us -> 77.9 us (0.981)
  Pallas kernels: 18.2 us -> 16.8 us
where the time goes in v5:
time: 77.9 us; the launch traced here: 77.6 us
  blocking collectives  58.9 us (76%)
  Pallas kernels  16.8 us (22%)
  waiting for transfers between devices  1.18 us (2%)
    all_to_all x2, blocking collectives, shards(): got = lax.all_to_all(pay, 'cell', 0, 0)  30.5 us
    all_to_all x2, blocking collectives, shards(): got = lax.all_to_all(pay, 'feat', 0, 0)  17 us
    all_to_all x1, blocking collectives, shards(): got = lax.all_to_all(pay, ('cyc', 'feat'), 0, 0)  11.5 us
    pallas_call x1, Pallas kernels, shards(): pl.pallas_call(contract_kernel, out_shape=(pltpu.VMEM((cells // 2, cycles...  8.21 us
    pallas_call x1, Pallas kernels, shards(): pl.pallas_call(functools.partial(cycles_kernel, float(cells * n_cell)), o...  4.72 us
    pallas_call x1, Pallas kernels, shards(): pl.pallas_call(cells_kernel, out_shape=(shape(rank, LANES), shape(rank, L...  1.9 us
  transfers between devices with their start and end apart: 1, of which 1 were waited for; matrix products, arithmetic and copies ran while one was open for 0% of the time, Pallas kernels for 0%

profile of v5, /device:TPU:0, one launch (start us, length us, event | category | flops | bytes accessed | tf_op | source)
XLA Modules:
  0.0 77.6 jit_solution(7034276882367631182)
XLA Ops:
  0.6 0.0 copy-start
  0.6 8.2 %contract.1 = (f32[64,256,128]{2,1,0:T(8,128)S(1)}, f32[128,256,128]{2,1,0:T(8,128)S(1)}, f32[8,48,128]{2,1,0:T(8,128)S(1)}) custom-call(s32[8,16]{1,0:T(8,128)} %present.1, f32[32,256]{1,0:T(8,128)} %bitcast.5, f32[32,128]{1,0:T(8,128)} %bitcast.7, f32[128,256,128]{2,1,0:T(8,128)} %tensor.1), custom_call_target="tpu_custom_call" | custom-call | tf_op jit(solution)/shard_map/contract/pallas_call | solution.py:317
  8.9 11.5 %all_to_all.25.got = f32[8,48,128]{2,1,0:T(8,128)S(1)} all-to-all(f32[8,48,128]{2,1,0:T(8,128)S(1)} %get-tuple-element.16), channel_id=1, replica_groups=mesh['cell'=16,'cyc'=2,'feat'=4] {'cyc','feat'}, dimensions={0} | all-to-all | bytes 393216 | tf_op jit(solution)/shard_map/all_to_all | solution.py:340
  20.3 1.9 %cells.1 = (f32[32,128]{1,0:T(8,128)S(1)}, f32[32,128]{1,0:T(8,128)S(1)}, f32[4,72,128]{2,1,0:T(8,128)S(1)}) custom-call(f32[8,48,128]{2,1,0:T(8,128)S(1)} %all_to_all.25.got, f32[64,256,128]{2,1,0:T(8,128)S(1)} %get-tuple-element.17.c_in), custom_call_target="tpu_custom_call" | custom-call | tf_op jit(solution)/shard_map/cells/pallas_call | solution.py:341
  22.2 8.9 %all_to_all.26.got = f32[4,72,128]{2,1,0:T(8,128)S(1)} all-to-all(f32[4,72,128]{2,1,0:T(8,128)S(1)} %get-tuple-element.18), channel_id=1, replica_groups=mesh['cell'=16,'cyc'=2,'feat'=4] {'feat'}, dimensions={0} | all-to-all | bytes 294912 | tf_op jit(solution)/shard_map/all_to_all | solution.py:350
  31.1 17.7 %all_to_all.27.got = f32[16,72,128]{2,1,0:T(8,128)S(1)} all-to-all(f32[16,72,128]{2,1,0:T(8,128)S(1)} %spread.1), channel_id=1, replica_groups=mesh['cell'=16,'cyc'=2,'feat'=4] {'cell'}, dimensions={0} | all-to-all | bytes 1179648 | tf_op jit(solution)/shard_map/all_to_all | solution.py:357
  48.9 0.0 copy-done
  48.9 4.7 %cycles.1 = (f32[32,128]{1,0:T(8,128)}, f32[32,256]{1,0:T(8,128)S(1)}, f32[32,128]{1,0:T(8,128)S(1)}, f32[40,128]{1,0:T(8,128)S(1)}) custom-call(s32[8,16]{1,0:T(8,128)S(1)} %copy-done, f32[16,72,128]{2,1,0:T(8,128)S(1)} %all_to_all.27.got, f32[32,128]{1,0:T(8,128)S(1)} %get-tuple-element.19.raw_cell, f32[32,128]{1,0:T(8,128)S(1)} %get-tuple-element.20.gram_feat, ...), custom_call_target="tpu_custom_call" | custom-call | tf_op jit(solution)/shard_map/cycles/pallas_call | solution.py:358
  53.6 0.1 collective-permute-start
  53.7 1.2 %collective-permute-done.other = f32[40,128]{1,0:T(8,128)S(1)} collective-permute-done((f32[40,128]{1,0:T(8,128)S(1)}, f32[40,128]{1,0:T(8,128)S(1)}, u32[]{:S(2)}, u32[]{:S(2)}) %collective-permute-start) | collective-permute-done | bytes 20512 | tf_op jit(solution)/shard_map/ppermute | solution.py:373
  54.9 12.7 %all_to_all.28.got = f32[16,40,128]{2,1,0:T(8,128)S(1)} all-to-all(f32[16,40,128]{2,1,0:T(8,128)S(1)} %pair.1), channel_id=1, replica_groups=mesh['cell'=16,'cyc'=2,'feat'=4] {'cell'}, dimensions={0} | all-to-all | bytes 655360 | tf_op jit(solution)/shard_map/all_to_all | solution.py:380
  67.6 1.2 %feats.1 = (f32[32,256]{1,0:T(8,128)}, f32[32,128]{1,0:T(8,128)S(1)}, f32[4,32,128]{2,1,0:T(8,128)S(1)}) custom-call(f32[16,40,128]{2,1,0:T(8,128)S(1)} %all_to_all.28.got, f32[32,256]{1,0:T(8,128)S(1)} %get-tuple-element.24.raw_cyc, f32[32,128]{1,0:T(8,128)S(1)} %get-tuple-element.25.unit_cell), custom_call_target="tpu_custom_call" | custom-call | tf_op jit(solution)/shard_map/feats/pallas_call | solution.py:381
  68.9 8.1 %all_to_all.29.got = f32[4,32,128]{2,1,0:T(8,128)S(1)} all-to-all(f32[4,32,128]{2,1,0:T(8,128)S(1)} %get-tuple-element.27), channel_id=1, replica_groups=mesh['cell'=16,'cyc'=2,'feat'=4] {'feat'}, dimensions={0} | all-to-all | bytes 131072 | tf_op jit(solution)/shard_map/all_to_all | solution.py:390
  77.0 0.6 last.1
  (2 shorter events, 0.1 us)
Async XLA Ops:
  0.6 48.2 %copy-start = (s32[8,16]{1,0:T(8,128)S(1)}, s32[8,16]{1,0:T(8,128)}, u32[]{:S(2)}) copy-start(s32[8,16]{1,0:T(8,128)} %present.1) | copy-start | bytes 1540
  53.6 1.3 %collective-permute-start = (f32[40,128]{1,0:T(8,128)S(1)}, f32[40,128]{1,0:T(8,128)S(1)}, u32[]{:S(2)}, u32[]{:S(2)}) collective-permute-start(f32[40,128]{1,0:T(8,128)S(1)} %get-tuple-element.23.mine), channel_id=1, source_target_pairs={{0,4},{4,0},{1,5},{5,1},{2,6},{6,2},{3,7},{7,3},{8,12},{12,8},{9,1... | collective-permute-start | bytes 61448 | tf_op jit(solution)/shard_map/ppermute | solution.py:373

commit v6 on v5

--- a/solution.py
+++ b/solution.py
@@ -221,7 +221,7 @@
 
 def cycles_kernel(
     cells_all, present, got, raw_cell, gram_feat, tensor,
-    cell_unit, raw_cyc_out, unit_out, pay, mask, raw_cyc, cell_buf, wide, sem,
+    cell_unit, raw_cyc_out, unit_out, pay, mask, raw_cyc, cell_buf, sem,
 ):
     cells = tensor.shape[0]
     chunks = cells // BLK
@@ -256,10 +256,10 @@
         left = jnp.concatenate([hi, lo], axis=0)
         for q in range(BLK):
             hi, lo = split(tensor[n * BLK + q])
-            wide[q] = dot(left, jnp.concatenate([hi, lo], axis=1), ((1,), (0,)))
-        for q in range(BLK):
-            w = wide[q, :rank, :LANES] + (wide[q, :rank, LANES:] + wide[q, rank:, :LANES])
-            acc = acc + w * rolled[:, q : q + 1]
+            high = dot(left, hi, ((1,), (0,)))
+            low = dot(left[:rank], lo, ((1,), (0,)))
+            one = rolled[:, q : q + 1]
+            acc = acc + (high[:rank] * one + (high[rank:] * one + low * one))
         return acc, pltpu.roll(rolled, LANES - BLK, 1)
 
     acc, _ = lax.fori_loop(0, chunks, step, (jnp.zeros((rank, LANES), F32), cell_t), unroll=4)
@@ -364,7 +364,6 @@
             pltpu.VMEM((chunks, cycles), F32),
             pltpu.VMEM((rank, cycles), F32),
             pltpu.VMEM((rank, cells), F32),
-            pltpu.VMEM((BLK, 2 * rank, 2 * feats), F32),
             pltpu.SemaphoreType.DMA((1,)),
         ],
         compiler_params=SMALL,

time: 77.9 us -> 77.5 us (level)
  no operation moved by 1% of the time
where the time goes in v6:
time: 77.5 us; the launch traced here: 77.2 us
  blocking collectives  58.9 us (76%)
  Pallas kernels  16.3 us (21%)
  waiting for transfers between devices  1.18 us (2%)
    all_to_all x2, blocking collectives, shards(): got = lax.all_to_all(pay, 'cell', 0, 0)  30.5 us
    all_to_all x2, blocking collectives, shards(): got = lax.all_to_all(pay, 'feat', 0, 0)  17 us
    all_to_all x1, blocking collectives, shards(): got = lax.all_to_all(pay, ('cyc', 'feat'), 0, 0)  11.5 us
    pallas_call x1, Pallas kernels, shards(): pl.pallas_call(contract_kernel, out_shape=(pltpu.VMEM((cells // 2, cycles...  8.21 us
    pallas_call x1, Pallas kernels, shards(): pl.pallas_call(functools.partial(cycles_kernel, float(cells * n_cell)), o...  4.28 us
    pallas_call x1, Pallas kernels, shards(): pl.pallas_call(cells_kernel, out_shape=(shape(rank, LANES), shape(rank, L...  1.9 us
  transfers between devices with their start and end apart: 1, of which 1 were waited for; matrix products, arithmetic and copies ran while one was open for 0% of the time, Pallas kernels for 0%

profile of v6, /device:TPU:0, one launch (start us, length us, event | category | flops | bytes accessed | tf_op | source)
XLA Modules:
  0.0 77.2 jit_solution(13090067881764064442)
XLA Ops:
  0.6 0.0 copy-start
  0.6 8.2 %contract.1 = (f32[64,256,128]{2,1,0:T(8,128)S(1)}, f32[128,256,128]{2,1,0:T(8,128)S(1)}, f32[8,48,128]{2,1,0:T(8,128)S(1)}) custom-call(s32[8,16]{1,0:T(8,128)} %present.1, f32[32,256]{1,0:T(8,128)} %bitcast.5, f32[32,128]{1,0:T(8,128)} %bitcast.7, f32[128,256,128]{2,1,0:T(8,128)} %tensor.1), custom_call_target="tpu_custom_call" | custom-call | tf_op jit(solution)/shard_map/contract/pallas_call | solution.py:317
  8.9 11.5 %all_to_all.25.got = f32[8,48,128]{2,1,0:T(8,128)S(1)} all-to-all(f32[8,48,128]{2,1,0:T(8,128)S(1)} %get-tuple-element.16), channel_id=1, replica_groups=mesh['cell'=16,'cyc'=2,'feat'=4] {'cyc','feat'}, dimensions={0} | all-to-all | bytes 393216 | tf_op jit(solution)/shard_map/all_to_all | solution.py:340
  20.3 1.9 %cells.1 = (f32[32,128]{1,0:T(8,128)S(1)}, f32[32,128]{1,0:T(8,128)S(1)}, f32[4,72,128]{2,1,0:T(8,128)S(1)}) custom-call(f32[8,48,128]{2,1,0:T(8,128)S(1)} %all_to_all.25.got, f32[64,256,128]{2,1,0:T(8,128)S(1)} %get-tuple-element.17.c_in), custom_call_target="tpu_custom_call" | custom-call | tf_op jit(solution)/shard_map/cells/pallas_call | solution.py:341
  22.2 8.9 %all_to_all.26.got = f32[4,72,128]{2,1,0:T(8,128)S(1)} all-to-all(f32[4,72,128]{2,1,0:T(8,128)S(1)} %get-tuple-element.18), channel_id=1, replica_groups=mesh['cell'=16,'cyc'=2,'feat'=4] {'feat'}, dimensions={0} | all-to-all | bytes 294912 | tf_op jit(solution)/shard_map/all_to_all | solution.py:350
  31.1 17.7 %all_to_all.27.got = f32[16,72,128]{2,1,0:T(8,128)S(1)} all-to-all(f32[16,72,128]{2,1,0:T(8,128)S(1)} %spread.1), channel_id=1, replica_groups=mesh['cell'=16,'cyc'=2,'feat'=4] {'cell'}, dimensions={0} | all-to-all | bytes 1179648 | tf_op jit(solution)/shard_map/all_to_all | solution.py:357
  48.9 0.0 copy-done
  48.9 4.3 %cycles.1 = (f32[32,128]{1,0:T(8,128)}, f32[32,256]{1,0:T(8,128)S(1)}, f32[32,128]{1,0:T(8,128)S(1)}, f32[40,128]{1,0:T(8,128)S(1)}) custom-call(s32[8,16]{1,0:T(8,128)S(1)} %copy-done, f32[16,72,128]{2,1,0:T(8,128)S(1)} %all_to_all.27.got, f32[32,128]{1,0:T(8,128)S(1)} %get-tuple-element.19.raw_cell, f32[32,128]{1,0:T(8,128)S(1)} %get-tuple-element.20.gram_feat, ...), custom_call_target="tpu_custom_call" | custom-call | tf_op jit(solution)/shard_map/cycles/pallas_call | solution.py:358
  53.2 0.1 collective-permute-start
  53.3 1.2 %collective-permute-done.other = f32[40,128]{1,0:T(8,128)S(1)} collective-permute-done((f32[40,128]{1,0:T(8,128)S(1)}, f32[40,128]{1,0:T(8,128)S(1)}, u32[]{:S(2)}, u32[]{:S(2)}) %collective-permute-start) | collective-permute-done | bytes 20512 | tf_op jit(solution)/shard_map/ppermute | solution.py:372
  54.5 12.7 %all_to_all.28.got = f32[16,40,128]{2,1,0:T(8,128)S(1)} all-to-all(f32[16,40,128]{2,1,0:T(8,128)S(1)} %pair.1), channel_id=1, replica_groups=mesh['cell'=16,'cyc'=2,'feat'=4] {'cell'}, dimensions={0} | all-to-all | bytes 655360 | tf_op jit(solution)/shard_map/all_to_all | solution.py:379
  67.2 1.2 %feats.1 = (f32[32,256]{1,0:T(8,128)}, f32[32,128]{1,0:T(8,128)S(1)}, f32[4,32,128]{2,1,0:T(8,128)S(1)}) custom-call(f32[16,40,128]{2,1,0:T(8,128)S(1)} %all_to_all.28.got, f32[32,256]{1,0:T(8,128)S(1)} %get-tuple-element.24.raw_cyc, f32[32,128]{1,0:T(8,128)S(1)} %get-tuple-element.25.unit_cell), custom_call_target="tpu_custom_call" | custom-call | tf_op jit(solution)/shard_map/feats/pallas_call | solution.py:380
  68.4 8.1 %all_to_all.29.got = f32[4,32,128]{2,1,0:T(8,128)S(1)} all-to-all(f32[4,32,128]{2,1,0:T(8,128)S(1)} %get-tuple-element.27), channel_id=1, replica_groups=mesh['cell'=16,'cyc'=2,'feat'=4] {'feat'}, dimensions={0} | all-to-all | bytes 131072 | tf_op jit(solution)/shard_map/all_to_all | solution.py:389
  76.5 0.6 last.1
  (2 shorter events, 0.1 us)
Async XLA Ops:
  0.6 48.2 %copy-start = (s32[8,16]{1,0:T(8,128)S(1)}, s32[8,16]{1,0:T(8,128)}, u32[]{:S(2)}) copy-start(s32[8,16]{1,0:T(8,128)} %present.1) | copy-start | bytes 1540
  53.2 1.3 %collective-permute-start = (f32[40,128]{1,0:T(8,128)S(1)}, f32[40,128]{1,0:T(8,128)S(1)}, u32[]{:S(2)}, u32[]{:S(2)}) collective-permute-start(f32[40,128]{1,0:T(8,128)S(1)} %get-tuple-element.23.mine), channel_id=1, source_target_pairs={{0,4},{4,0},{1,5},{5,1},{2,6},{6,2},{3,7},{7,3},{8,12},{12,8},{9,1... | collective-permute-start | bytes 61448 | tf_op jit(solution)/shard_map/ppermute | solution.py:372
